TPU v7x, 32 devices: a whole 2x2x4 slice. The times are simulated.
32 devices in a mesh: groups: 2 (over y), ctx: 4 (over z), head: 4 (over x, core).
Axes of the slice: x: 2, y: 2, z: 4, core: 2. Of those that a mesh axis runs over, the one named last changes fastest.
Arguments:
- queries: bfloat16 [2048, 4096], P(('groups', 'ctx'), 'head'), parts along dimension 0, may hold values from -250 to 250
- rotated_key_rows: bfloat16 [2048, 1024], P(('groups', 'ctx'), 'head'), parts along dimension 0, may hold values from -6 to 6
- value_state_rows: bfloat16 [2048, 1024], P(('groups', 'ctx'), 'head'), parts along dimension 0, may hold values from -6 to 6
- retained_positions: int32 [8, 32], P(('groups', 'ctx')), parts along dimension 0, may hold values from 0 to 255, as said below
- anchor_length: int32 [2], P('groups'), parts along dimension 0, may hold values from 1 to 128
- out_proj: bfloat16 [4096, 4096], P('head'), may hold values from -0.125 to 0.125
Outputs:
- attn_out: bfloat16 [2048, 4096], P(('groups', 'ctx'), 'head'), parts along dimension 0
There are 2 independent parts, one for each index of `groups`. A program takes and returns all parts, laid end to end along the dimension named above; an argument that names none is the same for every part. Nothing has to cross between parts.
Inputs may be any that keep to these rules, and one draw needn't show every extreme that they name: `retained_positions`: each row holds 32 different positions in increasing order.
All inputs are finite; a program needn't handle non-finite values.
Results may differ from a plain program's by a relative error of at most 0.015.
Values may be sent and summed in bfloat16 or wider, within the bound.
A program may use at most 64 MiB of HBM per device.

v0:
```python
import jax
import jax.numpy as jnp
from jax import lax
from jax.sharding import PartitionSpec as P

HEAD_SIZE = 128
ANCHOR = 128
RETAINED_COUNT = 32


def spread(value, axis, source):
    kept = jnp.where(lax.axis_index(axis) == source, value, 0).astype(value.dtype)
    return lax.psum(kept, axis)


def local(queries, rotated_key_rows, value_state_rows, retained_positions, anchor_length, out_proj):
    tok_rows = queries.shape[0]
    kv_heads = rotated_key_rows.shape[1] // HEAD_SIZE
    queries_per_key_head = queries.shape[1] // rotated_key_rows.shape[1]
    inv_root = HEAD_SIZE ** (-0.5)
    my_host = lax.axis_index("ctx")
    heads_q = queries.reshape(tok_rows, kv_heads, queries_per_key_head, HEAD_SIZE)
    places = jnp.arange(tok_rows, dtype=jnp.int32)

    def absorb(running, key_rows, val_rows, allowed):
        maxima, totals, numerator = running
        key_count = key_rows.shape[0]
        key_heads = key_rows.reshape(key_count, kv_heads, HEAD_SIZE)
        val_heads = val_rows.reshape(key_count, kv_heads, HEAD_SIZE)
        scores = (
            jnp.einsum("tkgd,nkd->kgtn", heads_q, key_heads, preferred_element_type=jnp.float32)
            * inv_root
        )
        scores = jnp.where(allowed, scores, -1e30)
        new_max = jnp.maximum(maxima, jnp.max(scores, axis=-1))
        weights = jnp.where(allowed, jnp.exp(scores - new_max[..., None]), 0.0)
        rescale = jnp.exp(maxima - new_max)
        totals = totals * rescale + jnp.sum(weights, axis=-1)
        numerator = numerator * rescale[..., None] + jnp.einsum(
            "kgtn,nkd->kgtd",
            weights.astype(jnp.bfloat16),
            val_heads,
            preferred_element_type=jnp.float32,
        )
        return (new_max, totals, numerator)

    running = (
        jnp.full((kv_heads, queries_per_key_head, tok_rows), -1e30, jnp.float32),
        jnp.zeros((kv_heads, queries_per_key_head, tok_rows), jnp.float32),
        jnp.zeros((kv_heads, queries_per_key_head, tok_rows, HEAD_SIZE), jnp.float32),
    )
    anchor_keys, anchor_vals = (
        spread(rotated_key_rows[:ANCHOR], "ctx", 0),
        spread(value_state_rows[:ANCHOR], "ctx", 0),
    )
    anchor_ok = ((jnp.arange(ANCHOR, dtype=jnp.int32) < anchor_length[0]) & (my_host > 0))[None, :]
    running = absorb(running, anchor_keys, anchor_vals, anchor_ok)
    kept_keys = rotated_key_rows[retained_positions[0]]
    kept_vals = value_state_rows[retained_positions[0]]
    passing_key_rows, passing_value_rows = (
        lax.all_gather(kept_keys, "ctx", axis=0, tiled=True),
        lax.all_gather(kept_vals, "ctx", axis=0, tiled=True),
    )
    key_total = passing_key_rows.shape[0]
    stride = min(key_total, 1024)
    block_len = min(stride, key_total)
    allowed = ((0 + jnp.arange(block_len, dtype=jnp.int32)) // RETAINED_COUNT < my_host)[None, :]
    running = absorb(running, passing_key_rows, passing_value_rows, allowed)
    local_ok = places[None, :] <= places[:, None]
    running = absorb(running, rotated_key_rows, value_state_rows, local_ok)
    maxima, totals, numerator = running
    attended = (
        (numerator / totals[..., None])
        .transpose(2, 0, 1, 3)
        .reshape(tok_rows, -1)
        .astype(jnp.bfloat16)
    )
    partial_value = jnp.dot(attended, out_proj, preferred_element_type=jnp.float32)
    return lax.psum_scatter(
        partial_value.astype(jnp.bfloat16), "head", scatter_dimension=1, tiled=True
    )


def solution(mesh):
    placed = (
        P(("groups", "ctx"), "head"),
        P(("groups", "ctx"), "head"),
        P(("groups", "ctx"), "head"),
        P(("groups", "ctx"), None),
        P("groups"),
        P("head", None),
    )
    return jax.shard_map(
        local, mesh=mesh, in_specs=placed, out_specs=P(("groups", "ctx"), "head"), check_vma=False
    )
```

profile of v0, /device:TPU:0, one launch (start us, length us, event | category | flops | bytes accessed | tf_op | source)
XLA Modules:
  0.0 95.7 jit_solution(15180239776846359299)
XLA Ops:
  6.5 0.9 slice.6
  7.4 0.1 copy.45
  7.6 0.7 copy.18
  8.3 1.0 %copy.20 = bf16[256,256]{0,1:T(8,128)(2,1)S(1)} copy(bf16[256,256]{1,0:T(8,128)(2,1)} %param.8) | data formatting | bytes 262144 | tf_op args[2]
  9.3 0.6 slice_select_fusion
  10.0 0.0 all-reduce.3.cloned.1.call-update
  10.0 0.0 reduce-scatter.2.cloned.1.call-start
  10.0 0.7 fusion.46
  10.7 1.5 %gather_fusion.1 = bf16[32,256]{1,0:T(8,128)(2,1)S(1)} fusion(bf16[256,256]{1,0:T(8,128)(2,1)} %param.8, s32[1024]{0:T(1024)S(1)} %pad_clamp_fusion), kind=kCustom, calls=%fused_computation.1 | custom fusion | bytes 32896 | tf_op jit(solution)/shard_map/gather | solution.py:59
  12.2 1.5 %gather_fusion = bf16[32,256]{1,0:T(8,128)(2,1)S(1)} fusion(bf16[256,256]{1,0:T(8,128)(2,1)} %param.7, s32[1024]{0:T(1024)S(1)} %pad_clamp_fusion), kind=kCustom, calls=%fused_computation | custom fusion | bytes 32896 | tf_op jit(solution)/shard_map/gather | solution.py:58
  13.8 0.9 reshape.107
  14.7 15.0 %all-gather = bf16[128,256]{1,0:T(8,128)(2,1)S(1)} all-gather(bf16[32,256]{1,0:T(8,128)(2,1)S(1)} %gather_fusion), channel_id=2, replica_groups=mesh['groups'=2,'ctx'=4,'head'=4] {'ctx'}, dimensions={0}, use_global_device_ids=true | all-gather | bytes 81920 | tf_op jit(solution)/shard_map/all_gather | solution.py:61
  29.7 0.1 copy.22
  29.9 0.4 reshape.103
  30.2 0.4 fusion.56
  30.6 0.4 copy-done
  31.0 1.5 %fusion = (f32[2,4,256]{2,1,0:T(4,128)S(1)}, f32[2,256,256,4]{2,1,3,0:T(8,128)S(1)}) fusion(pred[256,256]{0,1:T(8,128)(4,1)S(1)} %iota_compare_fusion, bf16[256,2,4,128]{3,2,1,0:T(4,128)(2,1)} %copy-done, bf16[256,2,128,1]{2,1,0,3:T(2,128)(2,1)S(1)} %bitcast.125), kind=kOutput, calls=%fused_computation.5 | convolution fusion | flops 135788544 | bytes 2826240 | tf_op jit(solution)/shard_map/tkgd,nkd->kgtn/dot_general | solution.py:31
  32.6 13.3 %all-gather.1 = bf16[128,256]{1,0:T(8,128)(2,1)S(1)} all-gather(bf16[32,256]{1,0:T(8,128)(2,1)S(1)} %gather_fusion.1), channel_id=3, replica_groups=mesh['groups'=2,'ctx'=4,'head'=4] {'ctx'}, dimensions={0}, use_global_device_ids=true | all-gather | bytes 81920 | tf_op jit(solution)/shard_map/all_gather | solution.py:62
  45.9 0.1 copy.25
  46.6 0.9 all-reduce.3.cloned.1.call-done
  47.6 1.4 %fusion.57 = (f32[2,4,256]{2,1,0:T(4,128)S(1)}, f32[2,4,256,128]{2,3,1,0:T(8,128)S(1)}) fusion(bf16[256,2,4,128]{3,2,1,0:T(4,128)(2,1)} %copy-done, bf16[128,2,128]{2,0,1:T(8,128)(2,1)} %get-tuple-element.5, pred[128]{0:T(512)(128)(4,1)S(1)} %compare_and_fusion), kind=kOutput, calls=%fused_computation.82 | convolution fusion | flops 67893248 | bytes 1646720 | tf_op jit(solution)/shard_map/tkgd,nkd->kgtn/dot_general | solution.py:31
  49.0 0.5 fusion.1
  49.5 0.4 convolution_bitcast_fusion
  49.9 0.5 fusion.20
  50.4 0.4 fusion.8
  50.8 0.0 slice-start.1
  50.8 0.7 fusion.13
  51.5 0.2 slice-done
  51.8 1.5 %slice-done.1 = s8[4194304]{0:T(1024)(128)(4,1)S(1)} async-done(((s8[8388608]{0:T(1024)(128)(4,1)}), s8[4194304]{0:T(1024)(128)(4,1)S(1)}, s32[]{:S(2)}) %slice-start.1) | async-done | bytes 4194328
  53.2 3.7 %convolution_convert_fusion = bf16[256,4096]{1,0:T(8,128)(2,1)} fusion(bf16[256,1024]{0,1:T(8,128)(2,1)S(1)} %bitcast.124, bf16[1024,4096]{1,0:T(8,128)(2,1)S(1)} %bitcast.123), kind=kOutput, calls=%fused_computation.2 | convolution fusion | flops 2148532224 | bytes 11010048 | tf_op jit(solution)/shard_map/dot_general | solution.py:78
  57.0 0.0 reduce-scatter.2.cloned.1.call-update
  57.0 31.8 %reduce-scatter.2.cloned.1.call-done = bf16[256,1024]{1,0:T(8,128)(2,1)} async-done(((bf16[256,4096]{1,0:T(8,128)(2,1)}), bf16[256,1024]{1,0:T(8,128)(2,1)}) %reduce-scatter.2.cloned.1.call-update) | async-done | bytes 524304 | tf_op jit(solution)/shard_map/reduce_scatter | solution.py:79
  (15 shorter events, 0.1 us)
Async XLA Ops:
  6.5 23.3 %copy-start.1 = (bf16[256,1024]{1,0:T(8,128)(2,1)S(1)}, bf16[256,1024]{1,0:T(8,128)(2,1)}, u32[]{:S(2)}) copy-start(bf16[256,1024]{1,0:T(8,128)(2,1)} %param.6) | copy-start | bytes 1572868
  6.5 41.0 %all-reduce.3.cloned.1.call-start = ((), (), s32[]{:S(2)}) async-start(), calls=%async_computation.2 | async-start | bytes 262144 | tf_op jit(solution)/shard_map/psum | solution.py:13
  10.0 78.8 %reduce-scatter.2.cloned.1.call-start = ((), (), s32[]{:S(2)}) async-start(), calls=%async_computation.1 | async-start | bytes 2621440 | tf_op jit(solution)/shard_map/reduce_scatter | solution.py:79
  30.2 0.8 copy-start
  49.5 0.9 copy-start.2
  49.5 2.2 %slice-start = ((s8[8388608]{0:T(1024)(128)(4,1)}), s8[4194304]{0:T(1024)(128)(4,1)S(1)}, s32[]{:S(2)}) async-start(s8[8388608]{0:T(1024)(128)(4,1)} %bitcast.122), calls=%async_computation.3 | async-start | bytes 8388608
  50.8 2.4 %slice-start.1 = ((s8[8388608]{0:T(1024)(128)(4,1)}), s8[4194304]{0:T(1024)(128)(4,1)S(1)}, s32[]{:S(2)}) async-start(s8[8388608]{0:T(1024)(128)(4,1)} %bitcast.122), calls=%async_computation.4 | async-start | bytes 8388608
Sparse Core Ops, SparseCore 0:
  10.1 37.4 all-reduce.2
  57.1 31.6 reduce-scatter.1
where the time goes:
time: 96 us; the launch traced here: 95.7 us
  waiting for transfers between devices  32.8 us (34%)
  blocking collectives  28.3 us (29%)
  between operations  14.2 us (15%)
  local copies, waits for them, and re-layouts  9.46 us (10%)
  matrix products  8.53 us (9%)
  other arithmetic  2.37 us (2%)
    reduce_scatter x1, waiting for transfers between devices, local(): lax.psum_scatter(partial_value.astype(jnp.bfloat16), 'head', scatter_dime...  31.8 us
    all_gather x1, blocking collectives, local(): lax.all_gather(kept_keys, 'ctx', axis=0, tiled=True)  15 us
    all_gather x1, blocking collectives, local(): lax.all_gather(kept_vals, 'ctx', axis=0, tiled=True)  13.3 us
    dot_general x1, matrix products, local(): jnp.dot(attended, out_proj, preferred_element_type=jnp.float32)  3.73 us
    dot_general x3, matrix products, absorb(): jnp.einsum('tkgd,nkd->kgtn', heads_q, key_heads, preferred_element_type=j...  3.33 us
    unnamed x12, local copies, waits for them, and re-layouts  3.25 us
  transfers between devices with their start and end apart: 2, of which 2 were waited for; matrix products, arithmetic and copies ran while one was open for 8% of the time, Pallas kernels for 0%

commit v1 on v0

v1 whole, which is shorter than its diff:
```python
import functools
import math

import jax
import jax.numpy as jnp
from jax import lax
from jax.experimental import pallas as pl
from jax.experimental.pallas import tpu as pltpu
from jax.sharding import PartitionSpec as P

HEAD_SIZE = 128
ANCHOR = 128
MESH = pl.DeviceIdType.MESH
NEG = -1e30
LAG = 3


def flip(index, mask):
    bit = 1
    while bit <= mask:
        if mask & bit:
            index = index + bit * (1 - 2 * ((index // bit) % 2))
        bit *= 2
    return index


def low_bit(r):
    return r & -r


def dot(a, b, dims=((1,), (0,))):
    return lax.dot_general(a, b, (dims, ((), ())), preferred_element_type=jnp.float32)


def kernel(
    n_ctx, n_head, pos_ref, len_ref, q_hbm, k_hbm, v_hbm, w_hbm, o_ref,
    q_v, kv_v, rem, w_v, acc_s, max_s, sum_s, att, part, outgoing, incoming,
    load_sem, w_sem, pass_send, pass_recv, anc_send, anc_recv, red_send, red_recv,
):
    me_c = lax.axis_index("ctx")
    me_h = lax.axis_index("head")
    tok, q_width = q_v.shape
    kv_width = kv_v.shape[1] // 2
    kv_heads = kv_width // HEAD_SIZE
    per_kv = q_width // kv_width
    retained = pos_ref.shape[1]
    rem_rows = rem.shape[0]
    chunks, _, chunk = part.shape[1:]
    slab = chunks * chunk
    half = tok // 2

    loads = [
        pltpu.make_async_copy(k_hbm, kv_v.at[:, pl.ds(0, kv_width)], load_sem.at[0]),
        pltpu.make_async_copy(v_hbm, kv_v.at[:, pl.ds(kv_width, kv_width)], load_sem.at[1]),
        pltpu.make_async_copy(q_hbm, q_v, load_sem.at[2]),
    ]
    for copy in loads:
        copy.start()

    rem[...] = jnp.zeros_like(rem)

    barrier = pltpu.get_barrier_semaphore()
    for j in range(n_ctx):
        @pl.when(me_c != j)
        def _():
            pl.semaphore_signal(barrier, inc=1, device_id={"ctx": j}, device_id_type=MESH)
    bit, steps = 1, 0
    while bit < n_head:
        pl.semaphore_signal(barrier, inc=1, device_id={"head": flip(me_h, bit)}, device_id_type=MESH)
        bit, steps = 2 * bit, steps + 1

    w_loads = {}
    for r in reversed(range(n_head)):
        columns = pl.ds(pl.multiple_of(flip(me_h, r) * slab, slab), slab)
        w_loads[r] = pltpu.make_async_copy(w_hbm.at[:, columns], w_v.at[r], w_sem.at[r])
        w_loads[r].start()

    loads[0].wait()
    loads[1].wait()
    picked = lax.broadcasted_iota(jnp.int32, (tok, retained), 0) == pos_ref[...]
    kept = dot(picked.astype(jnp.bfloat16), kv_v[...], ((0,), (0,)))
    mine = pl.ds(pl.multiple_of(ANCHOR + me_c * retained, retained), retained)
    rem[mine, :] = kept.astype(jnp.bfloat16)

    pl.semaphore_wait(barrier, n_ctx - 1 + steps)

    def pass_copy(source, target):
        rows = pl.ds(pl.multiple_of(ANCHOR + source * retained, retained), retained)
        return pltpu.make_async_remote_copy(
            src_ref=rem.at[rows, :], dst_ref=rem.at[rows, :],
            send_sem=pass_send.at[target], recv_sem=pass_recv.at[source],
            device_id={"ctx": target}, device_id_type=MESH,
        )

    def anchor_copy(target):
        return pltpu.make_async_remote_copy(
            src_ref=kv_v.at[pl.ds(0, ANCHOR), :], dst_ref=rem.at[pl.ds(0, ANCHOR), :],
            send_sem=anc_send.at[target], recv_sem=anc_recv,
            device_id={"ctx": target}, device_id_type=MESH,
        )

    for j in reversed(range(1, n_ctx)):
        @pl.when(me_c == 0)
        def _():
            anchor_copy(j).start()
    for j in reversed(range(1, n_ctx)):
        @pl.when(me_c < j)
        def _():
            pass_copy(me_c, j).start()

    scale = HEAD_SIZE ** -0.5 * math.log2(math.e)
    loads[2].wait()

    causal = jnp.where(
        lax.broadcasted_iota(jnp.int32, (half, half), 1)
        <= lax.broadcasted_iota(jnp.int32, (half, half), 0),
        0.0, NEG,
    )
    for h in range(kv_heads * per_kv):
        lanes = slice(h * HEAD_SIZE, (h + 1) * HEAD_SIZE)
        k = h // per_kv
        key_lanes = slice(k * HEAD_SIZE, (k + 1) * HEAD_SIZE)
        val_lanes = slice(kv_width + k * HEAD_SIZE, kv_width + (k + 1) * HEAD_SIZE)
        for top in (0, 1):
            rows = slice(top * half, (top + 1) * half)
            query = q_v[rows, lanes]
            s = dot(query, kv_v[rows, key_lanes], ((1,), (1,))) * scale + causal
            best = jnp.max(s, axis=1, keepdims=True)
            if top:
                s0 = dot(query, kv_v[0:half, key_lanes], ((1,), (1,))) * scale
                best = jnp.maximum(best, jnp.max(s0, axis=1, keepdims=True))
            p = jnp.exp2(s - best)
            total = jnp.sum(p, axis=1, keepdims=True)
            value = dot(p.astype(jnp.bfloat16), kv_v[rows, val_lanes])
            if top:
                p0 = jnp.exp2(s0 - best)
                total = total + jnp.sum(p0, axis=1, keepdims=True)
                value = value + dot(p0.astype(jnp.bfloat16), kv_v[0:half, val_lanes])
            acc_s[rows, lanes] = value
            max_s[h, rows, :] = best
            sum_s[h, rows, :] = total

    for j in range(n_ctx - 1):
        @pl.when(me_c > j)
        def _():
            pass_copy(j, me_c).wait_recv()

    @pl.when(me_c > 0)
    def _():
        anchor_copy(me_c).wait_recv()

    place = lax.broadcasted_iota(jnp.int32, (1, rem_rows), 1)
    seen_anchor = (place < jnp.minimum(len_ref[0], ANCHOR)) & (me_c > 0)
    seen_pass = (place >= ANCHOR) & (place - ANCHOR < me_c * retained)
    bias = jnp.where(seen_anchor | seen_pass, 0.0, NEG)
    for h in range(kv_heads * per_kv):
        lanes = slice(h * HEAD_SIZE, (h + 1) * HEAD_SIZE)
        k = h // per_kv
        key_lanes = slice(k * HEAD_SIZE, (k + 1) * HEAD_SIZE)
        val_lanes = slice(kv_width + k * HEAD_SIZE, kv_width + (k + 1) * HEAD_SIZE)
        for top in (0, 1):
            rows = slice(top * half, (top + 1) * half)
            s = dot(q_v[rows, lanes], rem[:, key_lanes], ((1,), (1,))) * scale + bias
            before = max_s[h, rows, :]
            best = jnp.maximum(before, jnp.max(s, axis=1, keepdims=True))
            p = jnp.exp2(s - best)
            fade = jnp.exp2(before - best)
            total = sum_s[h, rows, :] * fade + jnp.sum(p, axis=1, keepdims=True)
            value = acc_s[rows, lanes] * fade + dot(p.astype(jnp.bfloat16), rem[:, val_lanes])
            att[rows, lanes] = (value / total).astype(jnp.bfloat16)

    def red_copy(r, c):
        return pltpu.make_async_remote_copy(
            src_ref=outgoing.at[r - 1, c], dst_ref=incoming.at[r - 1, c],
            send_sem=red_send.at[r - 1, c], recv_sem=red_recv.at[r - 1, c],
            device_id={"head": flip(me_h, low_bit(r))}, device_id_type=MESH,
        )

    def finish(r, c):
        total = part[r, c]
        bit = 1
        while bit < (low_bit(r) if r else n_head):
            red_copy(r + bit, c).wait_recv()
            total = total + incoming[r + bit - 1, c].astype(jnp.float32)
            bit *= 2
        if r:
            outgoing[r - 1, c] = total.astype(jnp.bfloat16)
            red_copy(r, c).start()
        else:
            o_ref[:, c * chunk:(c + 1) * chunk] = total.astype(jnp.bfloat16)

    middle = n_head // 2
    units = [(r, c) for c in range(chunks) for r in reversed(range(middle, n_head))]
    units += [(r, c) for c in range(chunks) for r in reversed(range(middle))]
    late = []
    loaded = set()
    for r, c in units:
        if r not in loaded:
            w_loads[r].wait()
            loaded.add(r)
        value = dot(att[...], w_v[r, :, c * chunk:(c + 1) * chunk])
        if r % 2:
            outgoing[r - 1, c] = value.astype(jnp.bfloat16)
            red_copy(r, c).start()
        else:
            part[r, c] = value
            late.append((r, c))
        while late and (len(late) > LAG or (r < middle and late[0][0] >= middle)):
            finish(*late.pop(0))
    for r, c in late:
        finish(r, c)

    for r, c in units:
        if r:
            red_copy(r, c).wait_send()
    for j in range(1, n_ctx):
        @pl.when(me_c < j)
        def _():
            pass_copy(me_c, j).wait_send()

        @pl.when(me_c == 0)
        def _():
            anchor_copy(j).wait_send()


def local(n_ctx, n_head, queries, rotated_key_rows, value_state_rows, retained_positions, anchor_length, out_proj):
    tok, q_width = queries.shape
    kv_width = rotated_key_rows.shape[1]
    heads = q_width // HEAD_SIZE
    retained = retained_positions.shape[1]
    rem_rows = ANCHOR + n_ctx * retained
    slab = out_proj.shape[1] // n_head
    chunk = math.gcd(slab, 256)
    chunks = slab // chunk
    dma = pltpu.SemaphoreType.DMA
    anywhere = pl.BlockSpec(memory_space=pl.ANY)
    return pl.pallas_call(
        functools.partial(kernel, n_ctx, n_head),
        out_shape=jax.ShapeDtypeStruct((tok, slab), jnp.bfloat16),
        in_specs=[
            pl.BlockSpec(memory_space=pltpu.VMEM),
            pl.BlockSpec(memory_space=pltpu.SMEM),
            anywhere, anywhere, anywhere, anywhere,
        ],
        out_specs=pl.BlockSpec(memory_space=pltpu.VMEM),
        scratch_shapes=[
            pltpu.VMEM((tok, q_width), jnp.bfloat16),
            pltpu.VMEM((tok, 2 * kv_width), jnp.bfloat16),
            pltpu.VMEM((rem_rows, 2 * kv_width), jnp.bfloat16),
            pltpu.VMEM((n_head, q_width, slab), jnp.bfloat16),
            pltpu.VMEM((tok, q_width), jnp.float32),
            pltpu.VMEM((heads, tok, 1), jnp.float32),
            pltpu.VMEM((heads, tok, 1), jnp.float32),
            pltpu.VMEM((tok, q_width), jnp.bfloat16),
            pltpu.VMEM((n_head, chunks, tok, chunk), jnp.float32),
            pltpu.VMEM((n_head - 1, chunks, tok, chunk), jnp.bfloat16),
            pltpu.VMEM((n_head - 1, chunks, tok, chunk), jnp.bfloat16),
            dma((3,)),
            dma((n_head,)),
            dma((n_ctx,)),
            dma((n_ctx,)),
            dma((n_ctx,)),
            dma,
            dma((n_head - 1, chunks)),
            dma((n_head - 1, chunks)),
        ],
        compiler_params=pltpu.CompilerParams(
            collective_id=0, has_side_effects=True, vmem_limit_bytes=48 * 1024 * 1024
        ),
    )(retained_positions, anchor_length, queries, rotated_key_rows, value_state_rows, out_proj)


def solution(mesh):
    placed = (
        P(("groups", "ctx"), "head"),
        P(("groups", "ctx"), "head"),
        P(("groups", "ctx"), "head"),
        P(("groups", "ctx"), None),
        P("groups"),
        P("head", None),
    )
    return jax.shard_map(
        functools.partial(local, mesh.shape["ctx"], mesh.shape["head"]),
        mesh=mesh, in_specs=placed, out_specs=P(("groups", "ctx"), "head"), check_vma=False,
    )
```

time: 96 us -> 40.8 us (0.42)
  the two profiles are of different devices: /device:TPU:0 before, /device:TPU:8 now
where the time goes in v1:
time: 40.8 us; the launch traced here: 40.6 us
  Pallas kernels  35.6 us (87%)
  local copies, waits for them, and re-layouts  4.29 us (11%)
  between operations  0.67 us (2%)
    pallas_call x1, Pallas kernels, local(): pl.pallas_call(functools.partial(kernel, n_ctx, n_head), out_shape=jax.Sh...  35.6 us
    unnamed x9, local copies, waits for them, and re-layouts  4.29 us

profile of v1, /device:TPU:8, one launch (start us, length us, event | category | flops | bytes accessed | tf_op | source)
XLA Modules:
  0.0 40.6 jit_solution(14399573982945721836)
XLA Ops:
  0.7 0.0 copy-start
  0.7 1.0 %copy-done = bf16[256,1024]{1,0:T(8,128)(2,1)S(1)} copy-done((bf16[256,1024]{1,0:T(8,128)(2,1)S(1)}, bf16[256,1024]{1,0:T(8,128)(2,1)}, u32[]{:S(2)}) %copy-start) | copy-done | bytes 524312
  1.7 0.0 copy-start.1
  1.7 0.9 %copy-done.1 = bf16[256,256]{1,0:T(8,128)(2,1)S(1)} copy-done((bf16[256,256]{1,0:T(8,128)(2,1)S(1)}, bf16[256,256]{1,0:T(8,128)(2,1)}, u32[]{:S(2)}) %copy-start.1) | copy-done | bytes 131096
  2.6 0.0 copy-start.2
  2.6 0.9 %copy-done.2 = bf16[256,256]{1,0:T(8,128)(2,1)S(1)} copy-done((bf16[256,256]{1,0:T(8,128)(2,1)S(1)}, bf16[256,256]{1,0:T(8,128)(2,1)}, u32[]{:S(2)}) %copy-start.2) | copy-done | bytes 131096
  3.5 0.0 copy-start.3
  3.5 0.7 %copy-done.3 = s32[1,32]{1,0:T(1,128)S(1)} copy-done((s32[1,32]{1,0:T(1,128)S(1)}, s32[1,32]{1,0:T(1,128)}, u32[]{:S(2)}) %copy-start.3) | copy-done | bytes 152
  4.2 35.6 %shard_map.64 = bf16[256,1024]{1,0:T(8,128)(2,1)S(1)} custom-call(s32[1,32]{1,0:T(1,128)S(1)} %copy-done.3, s32[1]{0:T(128)S(6)} %copy.8.len_ref, bf16[256,1024]{1,0:T(8,128)(2,1)S(1)} %copy-done, bf16[256,256]{1,0:T(8,128)(2,1)S(1)} %copy-done.1, bf16[256,256]{1,0:T(8,128)(2,1)S(1)} %copy-done.2, bf16[1024,4096]{1,0:T(8,128)(2,1)} %w_hbm.1), custom_call_target="tpu_custom_call" | custom-call | tf_op jit(solution)/shard_map/pallas_call | solution.py:237
  39.8 0.8 %copy.9 = bf16[256,1024]{1,0:T(8,128)(2,1)} copy(bf16[256,1024]{1,0:T(8,128)(2,1)S(1)} %shard_map.64) | data formatting | bytes 1048576
Async XLA Ops:
  0.7 1.0 %copy-start = (bf16[256,1024]{1,0:T(8,128)(2,1)S(1)}, bf16[256,1024]{1,0:T(8,128)(2,1)}, u32[]{:S(2)}) copy-start(bf16[256,1024]{1,0:T(8,128)(2,1)} %q_hbm.1) | copy-start | bytes 1572868
  1.7 0.9 %copy-start.1 = (bf16[256,256]{1,0:T(8,128)(2,1)S(1)}, bf16[256,256]{1,0:T(8,128)(2,1)}, u32[]{:S(2)}) copy-start(bf16[256,256]{1,0:T(8,128)(2,1)} %k_hbm.1) | copy-start | bytes 393220
  2.6 0.9 %copy-start.2 = (bf16[256,256]{1,0:T(8,128)(2,1)S(1)}, bf16[256,256]{1,0:T(8,128)(2,1)}, u32[]{:S(2)}) copy-start(bf16[256,256]{1,0:T(8,128)(2,1)} %v_hbm.1) | copy-start | bytes 393220
  3.5 0.7 %copy-start.3 = (s32[1,32]{1,0:T(1,128)S(1)}, s32[1,32]{1,0:T(1,128)}, u32[]{:S(2)}) copy-start(s32[1,32]{1,0:T(1,128)} %pos_ref.1) | copy-start | bytes 388

commit v2 on v1

v2 whole, which is shorter than its diff:
```python
import functools
import math

import jax
import jax.numpy as jnp
from jax import lax
from jax.experimental import pallas as pl
from jax.experimental.pallas import tpu as pltpu
from jax.sharding import PartitionSpec as P

HEAD_SIZE = 128
ANCHOR = 128
MESH = pl.DeviceIdType.MESH
NEG = -1e30
LAG = 1
PIECES = 4


def flip(index, mask):
    bit = 1
    while bit <= mask:
        if mask & bit:
            index = index + bit * (1 - 2 * ((index // bit) % 2))
        bit *= 2
    return index


def low_bit(r):
    return r & -r


def dot(a, b, dims=((1,), (0,))):
    return lax.dot_general(a, b, (dims, ((), ())), preferred_element_type=jnp.float32)


def kernel(
    n_ctx, n_head, len_ref, pos_hbm, q_hbm, k_hbm, v_hbm, w_hbm, o_ref,
    pos_v, q_v, kv_v, rem, w_v, acc_s, max_s, sum_s, att, part, outgoing, incoming,
    load_sem, w_sem, pass_send, pass_recv, anc_send, anc_recv, red_send, red_recv,
):
    me_c = lax.axis_index("ctx")
    me_h = lax.axis_index("head")
    tok, q_width = q_v.shape
    kv_width = kv_v.shape[1] // 2
    kv_heads = kv_width // HEAD_SIZE
    per_kv = q_width // kv_width
    retained = pos_v.shape[1]
    rem_rows = rem.shape[0]
    chunks, _, chunk = part.shape
    slab = chunks * chunk
    half = tok // 2
    pieces = anc_recv.shape[0]
    piece = ANCHOR // pieces

    loads = [
        pltpu.make_async_copy(k_hbm, kv_v.at[:, pl.ds(0, kv_width)], load_sem.at[0]),
        pltpu.make_async_copy(v_hbm, kv_v.at[:, pl.ds(kv_width, kv_width)], load_sem.at[1]),
        pltpu.make_async_copy(pos_hbm, pos_v, load_sem.at[2]),
        pltpu.make_async_copy(q_hbm, q_v, load_sem.at[3]),
    ]
    for copy in loads:
        copy.start()

    rem[...] = jnp.zeros_like(rem)

    barrier = pltpu.get_barrier_semaphore()
    for j in range(n_ctx):
        @pl.when(me_c != j)
        def _():
            pl.semaphore_signal(barrier, inc=1, device_id={"ctx": j}, device_id_type=MESH)
    bit, steps = 1, 0
    while bit < n_head:
        pl.semaphore_signal(barrier, inc=1, device_id={"head": flip(me_h, bit)}, device_id_type=MESH)
        bit, steps = 2 * bit, steps + 1

    w_loads = {}
    for r in reversed(range(n_head)):
        columns = pl.ds(pl.multiple_of(flip(me_h, r) * slab, slab), slab)
        w_loads[r] = pltpu.make_async_copy(w_hbm.at[:, columns], w_v.at[r], w_sem.at[r])
        w_loads[r].start()

    def pass_copy(source, target):
        rows = pl.ds(pl.multiple_of(ANCHOR + source * retained, retained), retained)
        return pltpu.make_async_remote_copy(
            src_ref=rem.at[rows, :], dst_ref=rem.at[rows, :],
            send_sem=pass_send.at[target], recv_sem=pass_recv.at[source],
            device_id={"ctx": target}, device_id_type=MESH,
        )

    def anchor_copy(i, origin):
        rows = pl.ds(i * piece, piece)
        return pltpu.make_async_remote_copy(
            src_ref=(kv_v if origin else rem).at[rows, :], dst_ref=rem.at[rows, :],
            send_sem=anc_send.at[i], recv_sem=anc_recv.at[i],
            device_id={"ctx": lax.rem(me_c + 1, n_ctx)}, device_id_type=MESH,
        )

    for copy in loads[:3]:
        copy.wait()
    pl.semaphore_wait(barrier, n_ctx - 1 + steps)

    if n_ctx > 1:
        @pl.when(me_c == 0)
        def _():
            for i in range(pieces):
                anchor_copy(i, True).start()

    picked = lax.broadcasted_iota(jnp.int32, (tok, retained), 0) == pos_v[...]
    kept = dot(picked.astype(jnp.bfloat16), kv_v[...], ((0,), (0,)))
    mine = pl.ds(pl.multiple_of(ANCHOR + me_c * retained, retained), retained)
    rem[mine, :] = kept.astype(jnp.bfloat16)
    for j in reversed(range(1, n_ctx)):
        @pl.when(me_c < j)
        def _():
            pass_copy(me_c, j).start()

    scale = HEAD_SIZE ** -0.5 * math.log2(math.e)
    loads[3].wait()

    causal = jnp.where(
        lax.broadcasted_iota(jnp.int32, (half, half), 1)
        <= lax.broadcasted_iota(jnp.int32, (half, half), 0),
        0.0, NEG,
    )
    causal = jnp.concatenate([causal] * per_kv, axis=0)

    def stacked(k, top):
        rows = slice(top * half, (top + 1) * half)
        return jnp.concatenate(
            [q_v[rows, h * HEAD_SIZE:(h + 1) * HEAD_SIZE] for h in range(k * per_kv, (k + 1) * per_kv)], axis=0
        )

    local_units = [(k, top) for top in (0, 1) for k in range(kv_heads)]
    for number, (k, top) in enumerate(local_units):
        key_lanes = slice(k * HEAD_SIZE, (k + 1) * HEAD_SIZE)
        val_lanes = slice(kv_width + k * HEAD_SIZE, kv_width + (k + 1) * HEAD_SIZE)
        rows = slice(top * half, (top + 1) * half)
        query = stacked(k, top)
        s = dot(query, kv_v[rows, key_lanes], ((1,), (1,))) * scale + causal
        best = jnp.max(s, axis=1, keepdims=True)
        if top:
            s0 = dot(query, kv_v[0:half, key_lanes], ((1,), (1,))) * scale
            best = jnp.maximum(best, jnp.max(s0, axis=1, keepdims=True))
        p = jnp.exp2(s - best)
        total = jnp.sum(p, axis=1, keepdims=True)
        value = dot(p.astype(jnp.bfloat16), kv_v[rows, val_lanes])
        if top:
            p0 = jnp.exp2(s0 - best)
            total = total + jnp.sum(p0, axis=1, keepdims=True)
            value = value + dot(p0.astype(jnp.bfloat16), kv_v[0:half, val_lanes])
        acc_s[k, top] = value
        max_s[k, top] = best
        sum_s[k, top] = total

        @pl.when((me_c > 0) & (me_c < n_ctx - 1))
        def _():
            for i in range(number * pieces // len(local_units), (number + 1) * pieces // len(local_units)):
                anchor_copy(i, False).wait_recv()
                anchor_copy(i, False).start()

    for j in range(n_ctx - 1):
        @pl.when(me_c > j)
        def _():
            pass_copy(j, me_c).wait_recv()

    if n_ctx > 1:
        @pl.when(me_c == n_ctx - 1)
        def _():
            for i in range(pieces):
                anchor_copy(i, False).wait_recv()

    place = lax.broadcasted_iota(jnp.int32, (1, rem_rows), 1)
    seen_anchor = (place < jnp.minimum(len_ref[0], ANCHOR)) & (me_c > 0)
    seen_pass = (place >= ANCHOR) & (place - ANCHOR < me_c * retained)
    bias = jnp.where(seen_anchor | seen_pass, 0.0, NEG)

    def attend(top):
        rows = slice(top * half, (top + 1) * half)
        for k in range(kv_heads):
            key_lanes = slice(k * HEAD_SIZE, (k + 1) * HEAD_SIZE)
            val_lanes = slice(kv_width + k * HEAD_SIZE, kv_width + (k + 1) * HEAD_SIZE)
            s = dot(stacked(k, top), rem[:, key_lanes], ((1,), (1,))) * scale + bias
            before = max_s[k, top]
            best = jnp.maximum(before, jnp.max(s, axis=1, keepdims=True))
            p = jnp.exp2(s - best)
            fade = jnp.exp2(before - best)
            total = sum_s[k, top] * fade + jnp.sum(p, axis=1, keepdims=True)
            value = acc_s[k, top] * fade + dot(p.astype(jnp.bfloat16), rem[:, val_lanes])
            value = (value / total).astype(jnp.bfloat16)
            for g in range(per_kv):
                h = k * per_kv + g
                att[rows, h * HEAD_SIZE:(h + 1) * HEAD_SIZE] = value[g * half:(g + 1) * half]

    def red_copy(r, c, top):
        rows = pl.ds(top * half, half)
        return pltpu.make_async_remote_copy(
            src_ref=outgoing.at[r - 1, c, rows, :], dst_ref=incoming.at[r - 1, c, rows, :],
            send_sem=red_send.at[r - 1, c, top], recv_sem=red_recv.at[r - 1, c, top],
            device_id={"head": flip(me_h, low_bit(r))}, device_id_type=MESH,
        )

    def product(r, c, rows):
        return dot(att[rows, :], w_v[r, :, c * chunk:(c + 1) * chunk])

    def with_received(total, r, c, top, first, last):
        bit = first
        while bit < last:
            red_copy(r + bit, c, top).wait_recv()
            total = total + incoming[r + bit - 1, c, top * half:(top + 1) * half, :].astype(jnp.float32)
            bit *= 2
        return total

    def send(total, r, c, top):
        outgoing[r - 1, c, top * half:(top + 1) * half, :] = total.astype(jnp.bfloat16)
        red_copy(r, c, top).start()

    middle = n_head // 2
    for r in range(middle, n_head):
        w_loads[r].wait()
    for top in (0, 1):
        rows = slice(top * half, (top + 1) * half)
        attend(top)
        late = []
        for c in range(chunks):
            for r in reversed(range(middle, n_head)):
                value = product(r, c, rows)
                if r % 2:
                    send(value, r, c, top)
                else:
                    late.append((value, r, c))
            while len(late) > LAG:
                value, r, d = late.pop(0)
                send(with_received(value, r, d, top, 1, low_bit(r)), r, d, top)
        for value, r, d in late:
            send(with_received(value, r, d, top, 1, low_bit(r)), r, d, top)

    for r in range(middle):
        w_loads[r].wait()
    for r in reversed(range(1, middle)):
        for c in range(chunks):
            value = product(r, c, slice(0, tok))
            for top in (0, 1):
                send(with_received(value[top * half:(top + 1) * half], r, c, top, 1, low_bit(r)), r, c, top)
    for c in range(chunks):
        part[c] = product(0, c, slice(0, tok))
    for c in range(chunks):
        for top in (0, 1):
            rows = slice(top * half, (top + 1) * half)
            part[c, rows, :] = with_received(part[c, rows, :], 0, c, top, 1, middle)
    for top in (0, 1):
        rows = slice(top * half, (top + 1) * half)
        for c in range(chunks):
            total = with_received(part[c, rows, :], 0, c, top, middle, n_head)
            o_ref[rows, c * chunk:(c + 1) * chunk] = total.astype(jnp.bfloat16)

    for r in range(1, n_head):
        for c in range(chunks):
            for top in (0, 1):
                red_copy(r, c, top).wait_send()
    for j in range(1, n_ctx):
        @pl.when(me_c < j)
        def _():
            pass_copy(me_c, j).wait_send()
    if n_ctx > 1:
        @pl.when(me_c < n_ctx - 1)
        def _():
            for i in range(pieces):
                anchor_copy(i, True).wait_send()


def local(n_ctx, n_head, queries, rotated_key_rows, value_state_rows, retained_positions, anchor_length, out_proj):
    tok, q_width = queries.shape
    kv_width = rotated_key_rows.shape[1]
    retained = retained_positions.shape[1]
    rem_rows = ANCHOR + n_ctx * retained
    slab = out_proj.shape[1] // n_head
    chunk = math.gcd(slab, 256)
    chunks = slab // chunk
    dma = pltpu.SemaphoreType.DMA
    held = pl.BlockSpec(memory_space=pltpu.HBM)
    per_kv = q_width // kv_width
    kv_heads = kv_width // HEAD_SIZE
    stack = per_kv * tok // 2
    return pl.pallas_call(
        functools.partial(kernel, n_ctx, n_head),
        out_shape=jax.ShapeDtypeStruct((tok, slab), jnp.bfloat16),
        in_specs=[pl.BlockSpec(memory_space=pltpu.SMEM), held, held, held, held, held],
        out_specs=pl.BlockSpec(memory_space=pltpu.VMEM),
        scratch_shapes=[
            pltpu.VMEM((1, retained), jnp.int32),
            pltpu.VMEM((tok, q_width), jnp.bfloat16),
            pltpu.VMEM((tok, 2 * kv_width), jnp.bfloat16),
            pltpu.VMEM((rem_rows, 2 * kv_width), jnp.bfloat16),
            pltpu.VMEM((n_head, q_width, slab), jnp.bfloat16),
            pltpu.VMEM((kv_heads, 2, stack, HEAD_SIZE), jnp.float32),
            pltpu.VMEM((kv_heads, 2, stack, 1), jnp.float32),
            pltpu.VMEM((kv_heads, 2, stack, 1), jnp.float32),
            pltpu.VMEM((tok, q_width), jnp.bfloat16),
            pltpu.VMEM((chunks, tok, chunk), jnp.float32),
            pltpu.VMEM((n_head - 1, chunks, tok, chunk), jnp.bfloat16),
            pltpu.VMEM((n_head - 1, chunks, tok, chunk), jnp.bfloat16),
            dma((4,)),
            dma((n_head,)),
            dma((n_ctx,)),
            dma((n_ctx,)),
            dma((PIECES,)),
            dma((PIECES,)),
            dma((n_head - 1, chunks, 2)),
            dma((n_head - 1, chunks, 2)),
        ],
        compiler_params=pltpu.CompilerParams(
            collective_id=0, has_side_effects=True, vmem_limit_bytes=48 * 1024 * 1024
        ),
    )(anchor_length, retained_positions, queries, rotated_key_rows, value_state_rows, out_proj)


def solution(mesh):
    placed = (
        P(("groups", "ctx"), "head"),
        P(("groups", "ctx"), "head"),
        P(("groups", "ctx"), "head"),
        P(("groups", "ctx"), None),
        P("groups"),
        P("head", None),
    )
    return jax.shard_map(
        functools.partial(local, mesh.shape["ctx"], mesh.shape["head"]),
        mesh=mesh, in_specs=placed, out_specs=P(("groups", "ctx"), "head"), check_vma=False,
    )
```

time: 40.8 us -> 36 us (0.88)
  the two profiles are of different devices: /device:TPU:8 before, /device:TPU:25 now
where the time goes in v2:
time: 36 us; the launch traced here: 35.8 us
  Pallas kernels  30.8 us (86%)
  local copies, waits for them, and re-layouts  4.29 us (12%)
  between operations  0.67 us (2%)
    pallas_call x1, Pallas kernels, local(): pl.pallas_call(functools.partial(kernel, n_ctx, n_head), out_shape=jax.Sh...  30.8 us
    unnamed x9, local copies, waits for them, and re-layouts  4.29 us

profile of v2, /device:TPU:25, one launch (start us, length us, event | category | flops | bytes accessed | tf_op | source)
XLA Modules:
  0.0 35.8 jit_solution(5032501607490314668)
XLA Ops:
  0.7 0.0 copy-start
  0.7 1.0 %copy-done = bf16[256,1024]{1,0:T(8,128)(2,1)S(1)} copy-done((bf16[256,1024]{1,0:T(8,128)(2,1)S(1)}, bf16[256,1024]{1,0:T(8,128)(2,1)}, u32[]{:S(2)}) %copy-start) | copy-done | bytes 524312
  1.7 0.0 copy-start.1
  1.7 0.9 %copy-done.1 = bf16[256,256]{1,0:T(8,128)(2,1)S(1)} copy-done((bf16[256,256]{1,0:T(8,128)(2,1)S(1)}, bf16[256,256]{1,0:T(8,128)(2,1)}, u32[]{:S(2)}) %copy-start.1) | copy-done | bytes 131096
  2.6 0.0 copy-start.2
  2.6 0.9 %copy-done.2 = bf16[256,256]{1,0:T(8,128)(2,1)S(1)} copy-done((bf16[256,256]{1,0:T(8,128)(2,1)S(1)}, bf16[256,256]{1,0:T(8,128)(2,1)}, u32[]{:S(2)}) %copy-start.2) | copy-done | bytes 131096
  3.5 0.0 copy-start.3
  3.5 0.7 %copy-done.3 = s32[1,32]{1,0:T(1,128)S(1)} copy-done((s32[1,32]{1,0:T(1,128)S(1)}, s32[1,32]{1,0:T(1,128)}, u32[]{:S(2)}) %copy-start.3) | copy-done | bytes 152
  4.2 30.8 %shard_map.64 = bf16[256,1024]{1,0:T(8,128)(2,1)S(1)} custom-call(s32[1]{0:T(128)S(6)} %copy.8.len_ref, s32[1,32]{1,0:T(1,128)S(1)} %copy-done.3, bf16[256,1024]{1,0:T(8,128)(2,1)S(1)} %copy-done, bf16[256,256]{1,0:T(8,128)(2,1)S(1)} %copy-done.1, bf16[256,256]{1,0:T(8,128)(2,1)S(1)} %copy-done.2, bf16[1024,4096]{1,0:T(8,128)(2,1)} %w_hbm.1), custom_call_target="tpu_custom_call" | custom-call | tf_op jit(solution)/shard_map/pallas_call | solution.py:284
  35.0 0.8 %copy.9 = bf16[256,1024]{1,0:T(8,128)(2,1)} copy(bf16[256,1024]{1,0:T(8,128)(2,1)S(1)} %shard_map.64) | data formatting | bytes 1048576
Async XLA Ops:
  0.7 1.0 %copy-start = (bf16[256,1024]{1,0:T(8,128)(2,1)S(1)}, bf16[256,1024]{1,0:T(8,128)(2,1)}, u32[]{:S(2)}) copy-start(bf16[256,1024]{1,0:T(8,128)(2,1)} %q_hbm.1) | copy-start | bytes 1572868
  1.7 0.9 %copy-start.1 = (bf16[256,256]{1,0:T(8,128)(2,1)S(1)}, bf16[256,256]{1,0:T(8,128)(2,1)}, u32[]{:S(2)}) copy-start(bf16[256,256]{1,0:T(8,128)(2,1)} %k_hbm.1) | copy-start | bytes 393220
  2.6 0.9 %copy-start.2 = (bf16[256,256]{1,0:T(8,128)(2,1)S(1)}, bf16[256,256]{1,0:T(8,128)(2,1)}, u32[]{:S(2)}) copy-start(bf16[256,256]{1,0:T(8,128)(2,1)} %v_hbm.1) | copy-start | bytes 393220
  3.5 0.7 %copy-start.3 = (s32[1,32]{1,0:T(1,128)S(1)}, s32[1,32]{1,0:T(1,128)}, u32[]{:S(2)}) copy-start(s32[1,32]{1,0:T(1,128)} %pos_hbm.1) | copy-start | bytes 388

commit v3 on v2

--- a/solution.py
+++ b/solution.py
@@ -13,7 +13,6 @@
 MESH = pl.DeviceIdType.MESH
 NEG = -1e30
 LAG = 1
-PIECES = 4
 
 
 def flip(index, mask):
@@ -35,33 +34,48 @@
 
 def kernel(
     n_ctx, n_head, len_ref, pos_hbm, q_hbm, k_hbm, v_hbm, w_hbm, o_ref,
-    pos_v, q_v, kv_v, rem, w_v, acc_s, max_s, sum_s, att, part, outgoing, incoming,
+    pos_v, q_v, k_v, v_v, rem_k, rem_v, w_v, acc_s, max_s, p_s, att, part, outgoing, incoming,
     load_sem, w_sem, pass_send, pass_recv, anc_send, anc_recv, red_send, red_recv,
 ):
     me_c = lax.axis_index("ctx")
     me_h = lax.axis_index("head")
     tok, q_width = q_v.shape
-    kv_width = kv_v.shape[1] // 2
+    kv_width = k_v.shape[1]
     kv_heads = kv_width // HEAD_SIZE
     per_kv = q_width // kv_width
     retained = pos_v.shape[1]
-    rem_rows = rem.shape[0]
+    rem_rows = rem_k.shape[0]
     chunks, _, chunk = part.shape
     slab = chunks * chunk
     half = tok // 2
-    pieces = anc_recv.shape[0]
-    piece = ANCHOR // pieces
-
-    loads = [
-        pltpu.make_async_copy(k_hbm, kv_v.at[:, pl.ds(0, kv_width)], load_sem.at[0]),
-        pltpu.make_async_copy(v_hbm, kv_v.at[:, pl.ds(kv_width, kv_width)], load_sem.at[1]),
-        pltpu.make_async_copy(pos_hbm, pos_v, load_sem.at[2]),
-        pltpu.make_async_copy(q_hbm, q_v, load_sem.at[3]),
+    pieces = 2 * kv_heads
+
+    def key_lanes(k):
+        return pl.ds(k * HEAD_SIZE, HEAD_SIZE)
+
+    def val_lanes(k):
+        return pl.ds(2 * k * HEAD_SIZE, HEAD_SIZE)
+
+    def val_wide(k):
+        return pl.ds(2 * k * HEAD_SIZE, 2 * HEAD_SIZE)
+
+    loads = [pltpu.make_async_copy(k_hbm, k_v, load_sem.at[0])]
+    loads += [
+        pltpu.make_async_copy(v_hbm.at[:, key_lanes(k)], v_v.at[:, val_lanes(k)], load_sem.at[3 + k])
+        for k in range(kv_heads)
     ]
+    loads.append(pltpu.make_async_copy(pos_hbm, pos_v, load_sem.at[1]))
+    load_q = pltpu.make_async_copy(q_hbm, q_v, load_sem.at[2])
     for copy in loads:
         copy.start()
-
-    rem[...] = jnp.zeros_like(rem)
+    load_q.start()
+
+    rem_k[...] = jnp.zeros_like(rem_k)
+    for k in range(kv_heads):
+        ones = slice((2 * k + 1) * HEAD_SIZE, (2 * k + 2) * HEAD_SIZE)
+        v_v[:, ones] = jnp.ones((tok, HEAD_SIZE), jnp.bfloat16)
+        rem_v[:, ones] = jnp.ones((rem_rows, HEAD_SIZE), jnp.bfloat16)
+        rem_v[:, val_lanes(k)] = jnp.zeros((rem_rows, HEAD_SIZE), jnp.bfloat16)
 
     barrier = pltpu.get_barrier_semaphore()
     for j in range(n_ctx):
@@ -79,23 +93,31 @@
         w_loads[r] = pltpu.make_async_copy(w_hbm.at[:, columns], w_v.at[r], w_sem.at[r])
         w_loads[r].start()
 
-    def pass_copy(source, target):
+    def pass_copies(source, target):
         rows = pl.ds(pl.multiple_of(ANCHOR + source * retained, retained), retained)
+        refs = [rem_k.at[rows, :]] + [rem_v.at[rows, val_lanes(k)] for k in range(kv_heads)]
+        return [
+            pltpu.make_async_remote_copy(
+                src_ref=ref, dst_ref=ref,
+                send_sem=pass_send.at[target, i], recv_sem=pass_recv.at[source, i],
+                device_id={"ctx": target}, device_id_type=MESH,
+            )
+            for i, ref in enumerate(refs)
+        ]
+
+    def anchor_copy(i, origin):
+        rows = pl.ds(0, ANCHOR)
+        if i < kv_heads:
+            source, target, lanes = k_v, rem_k, key_lanes(i)
+        else:
+            source, target, lanes = v_v, rem_v, val_lanes(i - kv_heads)
         return pltpu.make_async_remote_copy(
-            src_ref=rem.at[rows, :], dst_ref=rem.at[rows, :],
-            send_sem=pass_send.at[target], recv_sem=pass_recv.at[source],
-            device_id={"ctx": target}, device_id_type=MESH,
-        )
-
-    def anchor_copy(i, origin):
-        rows = pl.ds(i * piece, piece)
-        return pltpu.make_async_remote_copy(
-            src_ref=(kv_v if origin else rem).at[rows, :], dst_ref=rem.at[rows, :],
+            src_ref=(source if origin else target).at[rows, lanes], dst_ref=target.at[rows, lanes],
             send_sem=anc_send.at[i], recv_sem=anc_recv.at[i],
             device_id={"ctx": lax.rem(me_c + 1, n_ctx)}, device_id_type=MESH,
         )
 
-    for copy in loads[:3]:
+    for copy in loads:
         copy.wait()
     pl.semaphore_wait(barrier, n_ctx - 1 + steps)
 
@@ -106,16 +128,19 @@
                 anchor_copy(i, True).start()
 
     picked = lax.broadcasted_iota(jnp.int32, (tok, retained), 0) == pos_v[...]
-    kept = dot(picked.astype(jnp.bfloat16), kv_v[...], ((0,), (0,)))
+    picked = picked.astype(jnp.bfloat16)
     mine = pl.ds(pl.multiple_of(ANCHOR + me_c * retained, retained), retained)
-    rem[mine, :] = kept.astype(jnp.bfloat16)
+    rem_k[mine, :] = dot(picked, k_v[...], ((0,), (0,))).astype(jnp.bfloat16)
+    for k in range(kv_heads):
+        rem_v[mine, val_lanes(k)] = dot(picked, v_v[:, val_lanes(k)], ((0,), (0,))).astype(jnp.bfloat16)
     for j in reversed(range(1, n_ctx)):
         @pl.when(me_c < j)
         def _():
-            pass_copy(me_c, j).start()
+            for copy in pass_copies(me_c, j):
+                copy.start()
 
     scale = HEAD_SIZE ** -0.5 * math.log2(math.e)
-    loads[3].wait()
+    load_q.wait()
 
     causal = jnp.where(
         lax.broadcasted_iota(jnp.int32, (half, half), 1)
@@ -130,63 +155,59 @@
             [q_v[rows, h * HEAD_SIZE:(h + 1) * HEAD_SIZE] for h in range(k * per_kv, (k + 1) * per_kv)], axis=0
         )
 
-    local_units = [(k, top) for top in (0, 1) for k in range(kv_heads)]
-    for number, (k, top) in enumerate(local_units):
-        key_lanes = slice(k * HEAD_SIZE, (k + 1) * HEAD_SIZE)
-        val_lanes = slice(kv_width + k * HEAD_SIZE, kv_width + (k + 1) * HEAD_SIZE)
+    units = [(k, top) for top in (0, 1) for k in range(kv_heads)]
+    for number, (k, top) in enumerate(units):
         rows = slice(top * half, (top + 1) * half)
         query = stacked(k, top)
-        s = dot(query, kv_v[rows, key_lanes], ((1,), (1,))) * scale + causal
+        s = dot(query, k_v[rows, key_lanes(k)], ((1,), (1,))) * scale + causal
         best = jnp.max(s, axis=1, keepdims=True)
         if top:
-            s0 = dot(query, kv_v[0:half, key_lanes], ((1,), (1,))) * scale
-            best = jnp.maximum(best, jnp.max(s0, axis=1, keepdims=True))
-        p = jnp.exp2(s - best)
-        total = jnp.sum(p, axis=1, keepdims=True)
-        value = dot(p.astype(jnp.bfloat16), kv_v[rows, val_lanes])
+            s0 = dot(query, k_v[0:half, key_lanes(k)], ((1,), (1,))) * scale
+            best = jnp.max(jnp.maximum(s, s0), axis=1, keepdims=True)
+        value = dot(jnp.exp2(s - best).astype(jnp.bfloat16), v_v[rows, val_wide(k)])
         if top:
-            p0 = jnp.exp2(s0 - best)
-            total = total + jnp.sum(p0, axis=1, keepdims=True)
-            value = value + dot(p0.astype(jnp.bfloat16), kv_v[0:half, val_lanes])
+            value = value + dot(jnp.exp2(s0 - best).astype(jnp.bfloat16), v_v[0:half, val_wide(k)])
         acc_s[k, top] = value
-        max_s[k, top] = best
-        sum_s[k, top] = total
+        max_s[k, top] = jnp.broadcast_to(best, max_s.shape[2:])
 
         @pl.when((me_c > 0) & (me_c < n_ctx - 1))
         def _():
-            for i in range(number * pieces // len(local_units), (number + 1) * pieces // len(local_units)):
+            for i in range(number * pieces // len(units), (number + 1) * pieces // len(units)):
                 anchor_copy(i, False).wait_recv()
                 anchor_copy(i, False).start()
 
-    for j in range(n_ctx - 1):
-        @pl.when(me_c > j)
-        def _():
-            pass_copy(j, me_c).wait_recv()
-
-    if n_ctx > 1:
-        @pl.when(me_c == n_ctx - 1)
-        def _():
-            for i in range(pieces):
-                anchor_copy(i, False).wait_recv()
-
+    def await_remote(first, last):
+        for j in range(n_ctx - 1):
+            @pl.when(me_c > j)
+            def _():
+                for copy in pass_copies(j, me_c)[(1 if first else 0):(1 + kv_heads if first else 1)]:
+                    copy.wait_recv()
+        if n_ctx > 1:
+            @pl.when(me_c == n_ctx - 1)
+            def _():
+                for i in range(first, last):
+                    anchor_copy(i, False).wait_recv()
+
+    await_remote(0, kv_heads)
     place = lax.broadcasted_iota(jnp.int32, (1, rem_rows), 1)
     seen_anchor = (place < jnp.minimum(len_ref[0], ANCHOR)) & (me_c > 0)
     seen_pass = (place >= ANCHOR) & (place - ANCHOR < me_c * retained)
     bias = jnp.where(seen_anchor | seen_pass, 0.0, NEG)
+    for k, top in units:
+        s = dot(stacked(k, top), rem_k[:, key_lanes(k)], ((1,), (1,))) * scale + bias
+        before = max_s[k, top]
+        best = jnp.maximum(before, jnp.max(s, axis=1, keepdims=True))
+        wide = jnp.concatenate([best] * (rem_rows // HEAD_SIZE), axis=1)
+        p_s[k, top] = jnp.exp2(s - wide).astype(jnp.bfloat16)
+        fade = jnp.exp2(before - best)
+        acc_s[k, top] = acc_s[k, top] * jnp.concatenate([fade, fade], axis=1)
+    await_remote(kv_heads, pieces)
 
     def attend(top):
         rows = slice(top * half, (top + 1) * half)
         for k in range(kv_heads):
-            key_lanes = slice(k * HEAD_SIZE, (k + 1) * HEAD_SIZE)
-            val_lanes = slice(kv_width + k * HEAD_SIZE, kv_width + (k + 1) * HEAD_SIZE)
-            s = dot(stacked(k, top), rem[:, key_lanes], ((1,), (1,))) * scale + bias
-            before = max_s[k, top]
-            best = jnp.maximum(before, jnp.max(s, axis=1, keepdims=True))
-            p = jnp.exp2(s - best)
-            fade = jnp.exp2(before - best)
-            total = sum_s[k, top] * fade + jnp.sum(p, axis=1, keepdims=True)
-            value = acc_s[k, top] * fade + dot(p.astype(jnp.bfloat16), rem[:, val_lanes])
-            value = (value / total).astype(jnp.bfloat16)
+            value = acc_s[k, top] + dot(p_s[k, top], rem_v[:, val_wide(k)])
+            value = (value[:, :HEAD_SIZE] / value[:, HEAD_SIZE:]).astype(jnp.bfloat16)
             for g in range(per_kv):
                 h = k * per_kv + g
                 att[rows, h * HEAD_SIZE:(h + 1) * HEAD_SIZE] = value[g * half:(g + 1) * half]
@@ -260,7 +281,8 @@
     for j in range(1, n_ctx):
         @pl.when(me_c < j)
         def _():
-            pass_copy(me_c, j).wait_send()
+            for copy in pass_copies(me_c, j):
+                copy.wait_send()
     if n_ctx > 1:
         @pl.when(me_c < n_ctx - 1)
         def _():
@@ -272,7 +294,7 @@
     tok, q_width = queries.shape
     kv_width = rotated_key_rows.shape[1]
     retained = retained_positions.shape[1]
-    rem_rows = ANCHOR + n_ctx * retained
+    rem_rows = pl.cdiv(ANCHOR + n_ctx * retained, HEAD_SIZE) * HEAD_SIZE
     slab = out_proj.shape[1] // n_head
     chunk = math.gcd(slab, 256)
     chunks = slab // chunk
@@ -281,6 +303,10 @@
     per_kv = q_width // kv_width
     kv_heads = kv_width // HEAD_SIZE
     stack = per_kv * tok // 2
+    operands = [
+        pltpu.with_memory_space_constraint(array, pltpu.HBM)
+        for array in (retained_positions, queries, rotated_key_rows, value_state_rows, out_proj)
+    ]
     return pl.pallas_call(
         functools.partial(kernel, n_ctx, n_head),
         out_shape=jax.ShapeDtypeStruct((tok, slab), jnp.bfloat16),
@@ -289,29 +315,31 @@
         scratch_shapes=[
             pltpu.VMEM((1, retained), jnp.int32),
             pltpu.VMEM((tok, q_width), jnp.bfloat16),
+            pltpu.VMEM((tok, kv_width), jnp.bfloat16),
             pltpu.VMEM((tok, 2 * kv_width), jnp.bfloat16),
+            pltpu.VMEM((rem_rows, kv_width), jnp.bfloat16),
             pltpu.VMEM((rem_rows, 2 * kv_width), jnp.bfloat16),
             pltpu.VMEM((n_head, q_width, slab), jnp.bfloat16),
+            pltpu.VMEM((kv_heads, 2, stack, 2 * HEAD_SIZE), jnp.float32),
             pltpu.VMEM((kv_heads, 2, stack, HEAD_SIZE), jnp.float32),
-            pltpu.VMEM((kv_heads, 2, stack, 1), jnp.float32),
-            pltpu.VMEM((kv_heads, 2, stack, 1), jnp.float32),
+            pltpu.VMEM((kv_heads, 2, stack, rem_rows), jnp.bfloat16),
             pltpu.VMEM((tok, q_width), jnp.bfloat16),
             pltpu.VMEM((chunks, tok, chunk), jnp.float32),
             pltpu.VMEM((n_head - 1, chunks, tok, chunk), jnp.bfloat16),
             pltpu.VMEM((n_head - 1, chunks, tok, chunk), jnp.bfloat16),
-            dma((4,)),
+            dma((3 + kv_heads,)),
             dma((n_head,)),
-            dma((n_ctx,)),
-            dma((n_ctx,)),
-            dma((PIECES,)),
-            dma((PIECES,)),
+            dma((n_ctx, 1 + kv_heads)),
+            dma((n_ctx, 1 + kv_heads)),
+            dma((2 * kv_heads,)),
+            dma((2 * kv_heads,)),
             dma((n_head - 1, chunks, 2)),
             dma((n_head - 1, chunks, 2)),
         ],
         compiler_params=pltpu.CompilerParams(
             collective_id=0, has_side_effects=True, vmem_limit_bytes=48 * 1024 * 1024
         ),
-    )(anchor_length, retained_positions, queries, rotated_key_rows, value_state_rows, out_proj)
+    )(anchor_length, *operands)
 
 
 def solution(mesh):

time: 36 us -> 31.5 us (0.88)
  local copies, waits for them, and re-layouts: 4.29 us -> 0.8 us
  Pallas kernels: 30.8 us -> 29.9 us
    unnamed x9 -> x1, local copies, waits for them, and re-layouts: 4.29 us -> 0.8 us
    pallas_call x1, Pallas kernels: 30.8 us -> 29.9 us  [local(): pl.pallas_call(functools.partial(kernel, n_ctx, n_head), out_shape=jax.Sh...]
where the time goes in v3:
time: 31.5 us; the launch traced here: 31.4 us
  Pallas kernels  29.9 us (95%)
  local copies, waits for them, and re-layouts  0.8 us (3%)
  between operations  0.66 us (2%)
    pallas_call x1, Pallas kernels, local(): pl.pallas_call(functools.partial(kernel, n_ctx, n_head), out_shape=jax.Sh...  29.9 us
    unnamed x1, local copies, waits for them, and re-layouts  0.8 us

profile of v3, /device:TPU:25, one launch (start us, length us, event | category | flops | bytes accessed | tf_op | source)
XLA Modules:
  0.0 31.4 jit_solution(6775862091677022615)
XLA Ops:
  0.7 29.9 %shard_map.64 = bf16[256,1024]{1,0:T(8,128)(2,1)S(1)} custom-call(s32[1]{0:T(128)S(6)} %copy.8.len_ref, s32[1,32]{1,0:T(1,128)} %pos_hbm.1, bf16[256,1024]{1,0:T(8,128)(2,1)} %q_hbm.1, bf16[256,256]{1,0:T(8,128)(2,1)} %k_hbm.1, bf16[256,256]{1,0:T(8,128)(2,1)} %v_hbm.1, bf16[1024,4096]{1,0:T(8,128)(2,1)} %w_hbm.1), custom_call_target="tpu_custom_call" | custom-call | tf_op jit(solution)/shard_map/pallas_call | solution.py:310
  30.6 0.8 %copy.9 = bf16[256,1024]{1,0:T(8,128)(2,1)} copy(bf16[256,1024]{1,0:T(8,128)(2,1)S(1)} %shard_map.64) | data formatting | bytes 1048576

commit v4 on v3

--- a/solution.py
+++ b/solution.py
@@ -78,10 +78,10 @@
         rem_v[:, val_lanes(k)] = jnp.zeros((rem_rows, HEAD_SIZE), jnp.bfloat16)
 
     barrier = pltpu.get_barrier_semaphore()
-    for j in range(n_ctx):
-        @pl.when(me_c != j)
-        def _():
-            pl.semaphore_signal(barrier, inc=1, device_id={"ctx": j}, device_id_type=MESH)
+    @pl.when(me_c > 0)
+    def _():
+        before = lax.rem(me_c + n_ctx - 1, n_ctx)
+        pl.semaphore_signal(barrier, inc=1, device_id={"ctx": before}, device_id_type=MESH)
     bit, steps = 1, 0
     while bit < n_head:
         pl.semaphore_signal(barrier, inc=1, device_id={"head": flip(me_h, bit)}, device_id_type=MESH)
@@ -93,14 +93,14 @@
         w_loads[r] = pltpu.make_async_copy(w_hbm.at[:, columns], w_v.at[r], w_sem.at[r])
         w_loads[r].start()
 
-    def pass_copies(source, target):
+    def pass_copies(source):
         rows = pl.ds(pl.multiple_of(ANCHOR + source * retained, retained), retained)
         refs = [rem_k.at[rows, :]] + [rem_v.at[rows, val_lanes(k)] for k in range(kv_heads)]
         return [
             pltpu.make_async_remote_copy(
                 src_ref=ref, dst_ref=ref,
-                send_sem=pass_send.at[target, i], recv_sem=pass_recv.at[source, i],
-                device_id={"ctx": target}, device_id_type=MESH,
+                send_sem=pass_send.at[source, i], recv_sem=pass_recv.at[source, i],
+                device_id={"ctx": lax.rem(me_c + 1, n_ctx)}, device_id_type=MESH,
             )
             for i, ref in enumerate(refs)
         ]
@@ -119,24 +119,40 @@
 
     for copy in loads:
         copy.wait()
-    pl.semaphore_wait(barrier, n_ctx - 1 + steps)
-
-    if n_ctx > 1:
-        @pl.when(me_c == 0)
-        def _():
-            for i in range(pieces):
-                anchor_copy(i, True).start()
-
+    @pl.when(me_c < n_ctx - 1)
+    def _():
+        pl.semaphore_wait(barrier, steps + 1)
+
+    @pl.when(me_c == n_ctx - 1)
+    def _():
+        pl.semaphore_wait(barrier, steps)
+
+    def start_anchor(first, last):
+        if n_ctx > 1:
+            @pl.when(me_c == 0)
+            def _():
+                for i in range(first, last):
+                    anchor_copy(i, True).start()
+
+    start_anchor(0, kv_heads)
     picked = lax.broadcasted_iota(jnp.int32, (tok, retained), 0) == pos_v[...]
     picked = picked.astype(jnp.bfloat16)
     mine = pl.ds(pl.multiple_of(ANCHOR + me_c * retained, retained), retained)
     rem_k[mine, :] = dot(picked, k_v[...], ((0,), (0,))).astype(jnp.bfloat16)
     for k in range(kv_heads):
         rem_v[mine, val_lanes(k)] = dot(picked, v_v[:, val_lanes(k)], ((0,), (0,))).astype(jnp.bfloat16)
-    for j in reversed(range(1, n_ctx)):
-        @pl.when(me_c < j)
+    @pl.when(me_c < n_ctx - 1)
+    def _():
+        for copy in pass_copies(me_c):
+            copy.start()
+
+    start_anchor(kv_heads, pieces)
+
+    def forward_pass(source):
+        @pl.when((me_c > source) & (me_c < n_ctx - 1))
         def _():
-            for copy in pass_copies(me_c, j):
+            for copy in pass_copies(source):
+                copy.wait_recv()
                 copy.start()
 
     scale = HEAD_SIZE ** -0.5 * math.log2(math.e)
@@ -170,38 +186,43 @@
         acc_s[k, top] = value
         max_s[k, top] = jnp.broadcast_to(best, max_s.shape[2:])
 
+        if number == 0:
+            for source in reversed(range(1, n_ctx - 1)):
+                forward_pass(source)
+
         @pl.when((me_c > 0) & (me_c < n_ctx - 1))
         def _():
-            for i in range(number * pieces // len(units), (number + 1) * pieces // len(units)):
-                anchor_copy(i, False).wait_recv()
-                anchor_copy(i, False).start()
-
-    def await_remote(first, last):
-        for j in range(n_ctx - 1):
-            @pl.when(me_c > j)
-            def _():
-                for copy in pass_copies(j, me_c)[(1 if first else 0):(1 + kv_heads if first else 1)]:
+            anchor_copy(number, False).wait_recv()
+            anchor_copy(number, False).start()
+
+        if number == kv_heads - 1 and n_ctx > 1:
+            forward_pass(0)
+
+    def await_remote(values):
+        @pl.when((me_c == n_ctx - 1) & (me_c > 0))
+        def _():
+            for source in range(n_ctx - 1):
+                copies = pass_copies(source)
+                for copy in copies[1:] if values else copies[:1]:
                     copy.wait_recv()
-        if n_ctx > 1:
-            @pl.when(me_c == n_ctx - 1)
-            def _():
-                for i in range(first, last):
-                    anchor_copy(i, False).wait_recv()
-
-    await_remote(0, kv_heads)
+            for k in range(kv_heads):
+                anchor_copy(k + values * kv_heads, False).wait_recv()
+
+    await_remote(0)
     place = lax.broadcasted_iota(jnp.int32, (1, rem_rows), 1)
     seen_anchor = (place < jnp.minimum(len_ref[0], ANCHOR)) & (me_c > 0)
     seen_pass = (place >= ANCHOR) & (place - ANCHOR < me_c * retained)
     bias = jnp.where(seen_anchor | seen_pass, 0.0, NEG)
-    for k, top in units:
-        s = dot(stacked(k, top), rem_k[:, key_lanes(k)], ((1,), (1,))) * scale + bias
-        before = max_s[k, top]
-        best = jnp.maximum(before, jnp.max(s, axis=1, keepdims=True))
-        wide = jnp.concatenate([best] * (rem_rows // HEAD_SIZE), axis=1)
-        p_s[k, top] = jnp.exp2(s - wide).astype(jnp.bfloat16)
-        fade = jnp.exp2(before - best)
-        acc_s[k, top] = acc_s[k, top] * jnp.concatenate([fade, fade], axis=1)
-    await_remote(kv_heads, pieces)
+
+    def weigh(top):
+        for k in range(kv_heads):
+            s = dot(stacked(k, top), rem_k[:, key_lanes(k)], ((1,), (1,))) * scale + bias
+            before = max_s[k, top]
+            best = jnp.maximum(before, jnp.max(s, axis=1, keepdims=True))
+            wide = jnp.concatenate([best] * (rem_rows // HEAD_SIZE), axis=1)
+            p_s[k, top] = jnp.exp2(s - wide).astype(jnp.bfloat16)
+            fade = jnp.exp2(before - best)
+            acc_s[k, top] = acc_s[k, top] * jnp.concatenate([fade, fade], axis=1)
 
     def attend(top):
         rows = slice(top * half, (top + 1) * half)
@@ -240,6 +261,9 @@
         w_loads[r].wait()
     for top in (0, 1):
         rows = slice(top * half, (top + 1) * half)
+        weigh(top)
+        if top == 0:
+            await_remote(1)
         attend(top)
         late = []
         for c in range(chunks):
@@ -278,16 +302,15 @@
         for c in range(chunks):
             for top in (0, 1):
                 red_copy(r, c, top).wait_send()
-    for j in range(1, n_ctx):
-        @pl.when(me_c < j)
+    @pl.when(me_c < n_ctx - 1)
+    def _():
+        for i in range(pieces):
+            anchor_copy(i, True).wait_send()
+    for source in range(n_ctx - 1):
+        @pl.when((me_c >= source) & (me_c < n_ctx - 1))
         def _():
-            for copy in pass_copies(me_c, j):
+            for copy in pass_copies(source):
                 copy.wait_send()
-    if n_ctx > 1:
-        @pl.when(me_c < n_ctx - 1)
-        def _():
-            for i in range(pieces):
-                anchor_copy(i, True).wait_send()
 
 
 def local(n_ctx, n_head, queries, rotated_key_rows, value_state_rows, retained_positions, anchor_length, out_proj):

time: 31.5 us -> 29.4 us (0.933)
  Pallas kernels: 29.9 us -> 27.8 us
    pallas_call x1, Pallas kernels: 29.9 us -> 27.8 us  [local(): pl.pallas_call(functools.partial(kernel, n_ctx, n_head), out_shape=jax.Sh...]
where the time goes in v4:
time: 29.4 us; the launch traced here: 29.2 us
  Pallas kernels  27.8 us (95%)
  local copies, waits for them, and re-layouts  0.8 us (3%)
  between operations  0.66 us (2%)
    pallas_call x1, Pallas kernels, local(): pl.pallas_call(functools.partial(kernel, n_ctx, n_head), out_shape=jax.Sh...  27.8 us
    unnamed x1, local copies, waits for them, and re-layouts  0.8 us

profile of v4, /device:TPU:25, one launch (start us, length us, event | category | flops | bytes accessed | tf_op | source)
XLA Modules:
  0.0 29.2 jit_solution(14044984260503945291)
XLA Ops:
  0.7 27.8 %shard_map.64 = bf16[256,1024]{1,0:T(8,128)(2,1)S(1)} custom-call(s32[1]{0:T(128)S(6)} %copy.8.len_ref, s32[1,32]{1,0:T(1,128)} %pos_hbm.1, bf16[256,1024]{1,0:T(8,128)(2,1)} %q_hbm.1, bf16[256,256]{1,0:T(8,128)(2,1)} %k_hbm.1, bf16[256,256]{1,0:T(8,128)(2,1)} %v_hbm.1, bf16[1024,4096]{1,0:T(8,128)(2,1)} %w_hbm.1), custom_call_target="tpu_custom_call" | custom-call | tf_op jit(solution)/shard_map/pallas_call | solution.py:333
  28.4 0.8 %copy.9 = bf16[256,1024]{1,0:T(8,128)(2,1)} copy(bf16[256,1024]{1,0:T(8,128)(2,1)S(1)} %shard_map.64) | data formatting | bytes 1048576

commit v5 on v4

--- a/solution.py
+++ b/solution.py
@@ -34,8 +34,8 @@
 
 def kernel(
     n_ctx, n_head, len_ref, pos_hbm, q_hbm, k_hbm, v_hbm, w_hbm, o_ref,
-    pos_v, q_v, k_v, v_v, rem_k, rem_v, w_v, acc_s, max_s, p_s, att, part, outgoing, incoming,
-    load_sem, w_sem, pass_send, pass_recv, anc_send, anc_recv, red_send, red_recv,
+    pos_v, q_v, k_v, v_v, rem_k, rem_v, w_v, acc_s, max_s, p_s, att, part, outgoing, incoming, relay,
+    load_sem, w_sem, pass_send, pass_recv, anc_send, anc_recv, red_send, red_recv, relay_send, relay_recv,
 ):
     me_c = lax.axis_index("ctx")
     me_h = lax.axis_index("head")
@@ -49,6 +49,8 @@
     slab = chunks * chunk
     half = tok // 2
     pieces = 2 * kv_heads
+    middle = n_head // 2
+    pairs = min(2, n_ctx // 2) if n_head > 1 else 0
 
     def key_lanes(k):
         return pl.ds(k * HEAD_SIZE, HEAD_SIZE)
@@ -86,6 +88,15 @@
     while bit < n_head:
         pl.semaphore_signal(barrier, inc=1, device_id={"head": flip(me_h, bit)}, device_id_type=MESH)
         bit, steps = 2 * bit, steps + 1
+    for i in range(pairs):
+        @pl.when(me_c == i)
+        def _():
+            pl.semaphore_signal(barrier, inc=1, device_id={"ctx": n_ctx - 1 - i}, device_id_type=MESH)
+
+        @pl.when(me_c == n_ctx - 1 - i)
+        def _():
+            other = {"ctx": i, "head": flip(me_h, middle)}
+            pl.semaphore_signal(barrier, inc=1, device_id=other, device_id_type=MESH)
 
     w_loads = {}
     for r in reversed(range(n_head)):
@@ -119,13 +130,12 @@
 
     for copy in loads:
         copy.wait()
-    @pl.when(me_c < n_ctx - 1)
-    def _():
-        pl.semaphore_wait(barrier, steps + 1)
-
-    @pl.when(me_c == n_ctx - 1)
-    def _():
-        pl.semaphore_wait(barrier, steps)
+    for j in range(n_ctx):
+        greeted = steps + (j < n_ctx - 1) + (j < pairs or j >= n_ctx - pairs)
+
+        @pl.when(me_c == j)
+        def _():
+            pl.semaphore_wait(barrier, greeted)
 
     def start_anchor(first, last):
         if n_ctx > 1:
@@ -241,6 +251,31 @@
             device_id={"head": flip(me_h, low_bit(r))}, device_id_type=MESH,
         )
 
+    def detours(i):
+        return [(c, 0) for c in range(1, min(chunks, 3 - i))]
+
+    def to_relay(i, c, top):
+        return pltpu.make_async_remote_copy(
+            src_ref=outgoing.at[middle - 1, c, pl.ds(top * half, half), :], dst_ref=relay.at[c - 1],
+            send_sem=red_send.at[middle - 1, c, top], recv_sem=relay_recv.at[c - 1],
+            device_id={"ctx": i}, device_id_type=MESH,
+        )
+
+    def from_relay(i, c, top):
+        return pltpu.make_async_remote_copy(
+            src_ref=relay.at[c - 1], dst_ref=incoming.at[middle - 1, c, pl.ds(top * half, half), :],
+            send_sem=relay_send.at[c - 1], recv_sem=red_recv.at[middle - 1, c, top],
+            device_id={"ctx": n_ctx - 1 - i, "head": flip(me_h, middle)}, device_id_type=MESH,
+        )
+
+    def pass_on():
+        for i in range(pairs):
+            @pl.when(me_c == i)
+            def _():
+                for c, top in detours(i):
+                    to_relay(i, c, top).wait_recv()
+                    from_relay(i, c, top).start()
+
     def product(r, c, rows):
         return dot(att[rows, :], w_v[r, :, c * chunk:(c + 1) * chunk])
 
@@ -254,9 +289,18 @@
 
     def send(total, r, c, top):
         outgoing[r - 1, c, top * half:(top + 1) * half, :] = total.astype(jnp.bfloat16)
-        red_copy(r, c, top).start()
-
-    middle = n_head // 2
+        takers = [i for i in range(pairs) if r == middle and (c, top) in detours(i)]
+        for i in takers:
+            @pl.when(me_c == n_ctx - 1 - i)
+            def _():
+                to_relay(i, c, top).start()
+        if takers:
+            @pl.when(me_c < n_ctx - len(takers))
+            def _():
+                red_copy(r, c, top).start()
+        else:
+            red_copy(r, c, top).start()
+
     for r in range(middle, n_head):
         w_loads[r].wait()
     for top in (0, 1):
@@ -295,6 +339,8 @@
     for top in (0, 1):
         rows = slice(top * half, (top + 1) * half)
         for c in range(chunks):
+            if top == 1 and c == chunks // 2:
+                pass_on()
             total = with_received(part[c, rows, :], 0, c, top, middle, n_head)
             o_ref[rows, c * chunk:(c + 1) * chunk] = total.astype(jnp.bfloat16)
 
@@ -302,6 +348,11 @@
         for c in range(chunks):
             for top in (0, 1):
                 red_copy(r, c, top).wait_send()
+    for i in range(pairs):
+        @pl.when(me_c == i)
+        def _():
+            for c, top in detours(i):
+                from_relay(i, c, top).wait_send()
     @pl.when(me_c < n_ctx - 1)
     def _():
         for i in range(pieces):
@@ -350,6 +401,7 @@
             pltpu.VMEM((chunks, tok, chunk), jnp.float32),
             pltpu.VMEM((n_head - 1, chunks, tok, chunk), jnp.bfloat16),
             pltpu.VMEM((n_head - 1, chunks, tok, chunk), jnp.bfloat16),
+            pltpu.VMEM((2, tok // 2, chunk), jnp.bfloat16),
             dma((3 + kv_heads,)),
             dma((n_head,)),
             dma((n_ctx, 1 + kv_heads)),
@@ -358,6 +410,8 @@
             dma((2 * kv_heads,)),
             dma((n_head - 1, chunks, 2)),
             dma((n_head - 1, chunks, 2)),
+            dma((2,)),
+            dma((2,)),
         ],
         compiler_params=pltpu.CompilerParams(
             collective_id=0, has_side_effects=True, vmem_limit_bytes=48 * 1024 * 1024

time: 29.4 us -> 33 us (1.12)
  Pallas kernels: 27.8 us -> 31.4 us
    pallas_call x1, Pallas kernels: 27.8 us -> 31.4 us  [local(): pl.pallas_call(functools.partial(kernel, n_ctx, n_head), out_shape=jax.Sh...]
where the time goes in v5:
time: 33 us; the launch traced here: 32.9 us
  Pallas kernels  31.4 us (95%)
  local copies, waits for them, and re-layouts  0.8 us (2%)
  between operations  0.66 us (2%)
    pallas_call x1, Pallas kernels, local(): pl.pallas_call(functools.partial(kernel, n_ctx, n_head), out_shape=jax.Sh...  31.4 us
    unnamed x1, local copies, waits for them, and re-layouts  0.8 us

profile of v5, /device:TPU:25, one launch (start us, length us, event | category | flops | bytes accessed | tf_op | source)
XLA Modules:
  0.0 32.9 jit_solution(15851051207191840928)
XLA Ops:
  0.7 31.4 %shard_map.64 = bf16[256,1024]{1,0:T(8,128)(2,1)S(1)} custom-call(s32[1]{0:T(128)S(6)} %copy.8.len_ref, s32[1,32]{1,0:T(1,128)} %pos_hbm.1, bf16[256,1024]{1,0:T(8,128)(2,1)} %q_hbm.1, bf16[256,256]{1,0:T(8,128)(2,1)} %k_hbm.1, bf16[256,256]{1,0:T(8,128)(2,1)} %v_hbm.1, bf16[1024,4096]{1,0:T(8,128)(2,1)} %w_hbm.1), custom_call_target="tpu_custom_call" | custom-call | tf_op jit(solution)/shard_map/pallas_call | solution.py:384
  32.1 0.8 %copy.9 = bf16[256,1024]{1,0:T(8,128)(2,1)} copy(bf16[256,1024]{1,0:T(8,128)(2,1)S(1)} %shard_map.64) | data formatting | bytes 1048576

commit v6 on v4

--- a/solution.py
+++ b/solution.py
@@ -108,17 +108,16 @@
     def anchor_copy(i, origin):
         rows = pl.ds(0, ANCHOR)
         if i < kv_heads:
-            source, target, lanes = k_v, rem_k, key_lanes(i)
+            source, target, lanes = k_hbm, rem_k, key_lanes(i)
         else:
-            source, target, lanes = v_v, rem_v, val_lanes(i - kv_heads)
+            source, target, lanes = v_hbm, rem_v, val_lanes(i - kv_heads)
+        held = target.at[rows, lanes]
         return pltpu.make_async_remote_copy(
-            src_ref=(source if origin else target).at[rows, lanes], dst_ref=target.at[rows, lanes],
+            src_ref=source.at[rows, key_lanes(i % kv_heads)] if origin else held, dst_ref=held,
             send_sem=anc_send.at[i], recv_sem=anc_recv.at[i],
             device_id={"ctx": lax.rem(me_c + 1, n_ctx)}, device_id_type=MESH,
         )
 
-    for copy in loads:
-        copy.wait()
     @pl.when(me_c < n_ctx - 1)
     def _():
         pl.semaphore_wait(barrier, steps + 1)
@@ -134,7 +133,9 @@
                 for i in range(first, last):
                     anchor_copy(i, True).start()
 
-    start_anchor(0, kv_heads)
+    start_anchor(0, pieces)
+    for copy in loads:
+        copy.wait()
     picked = lax.broadcasted_iota(jnp.int32, (tok, retained), 0) == pos_v[...]
     picked = picked.astype(jnp.bfloat16)
     mine = pl.ds(pl.multiple_of(ANCHOR + me_c * retained, retained), retained)
@@ -146,8 +147,6 @@
         for copy in pass_copies(me_c):
             copy.start()
 
-    start_anchor(kv_heads, pieces)
-
     def forward_pass(source):
         @pl.when((me_c > source) & (me_c < n_ctx - 1))
         def _():
@@ -173,6 +172,18 @@
 
     units = [(k, top) for top in (0, 1) for k in range(kv_heads)]
     for number, (k, top) in enumerate(units):
+        if number == 0:
+            for source in reversed(range(1, n_ctx - 1)):
+                forward_pass(source)
+
+        @pl.when((me_c > 0) & (me_c < n_ctx - 1))
+        def _():
+            anchor_copy(number, False).wait_recv()
+            anchor_copy(number, False).start()
+
+        if number == kv_heads - 1 and n_ctx > 1:
+            forward_pass(0)
+
         rows = slice(top * half, (top + 1) * half)
         query = stacked(k, top)
         s = dot(query, k_v[rows, key_lanes(k)], ((1,), (1,))) * scale + causal
@@ -185,18 +196,6 @@
             value = value + dot(jnp.exp2(s0 - best).astype(jnp.bfloat16), v_v[0:half, val_wide(k)])
         acc_s[k, top] = value
         max_s[k, top] = jnp.broadcast_to(best, max_s.shape[2:])
-
-        if number == 0:
-            for source in reversed(range(1, n_ctx - 1)):
-                forward_pass(source)
-
-        @pl.when((me_c > 0) & (me_c < n_ctx - 1))
-        def _():
-            anchor_copy(number, False).wait_recv()
-            anchor_copy(number, False).start()
-
-        if number == kv_heads - 1 and n_ctx > 1:
-            forward_pass(0)
 
     def await_remote(values):
         @pl.when((me_c == n_ctx - 1) & (me_c > 0))

time: 29.4 us -> 30.1 us (1.024)
  Pallas kernels: 27.8 us -> 28.5 us
    pallas_call x1, Pallas kernels: 27.8 us -> 28.5 us  [local(): pl.pallas_call(functools.partial(kernel, n_ctx, n_head), out_shape=jax.Sh...]
where the time goes in v6:
time: 30.1 us; the launch traced here: 29.9 us
  Pallas kernels  28.5 us (95%)
  local copies, waits for them, and re-layouts  0.8 us (3%)
  between operations  0.66 us (2%)
    pallas_call x1, Pallas kernels, local(): pl.pallas_call(functools.partial(kernel, n_ctx, n_head), out_shape=jax.Sh...  28.5 us
    unnamed x1, local copies, waits for them, and re-layouts  0.8 us

profile of v6, /device:TPU:25, one launch (start us, length us, event | category | flops | bytes accessed | tf_op | source)
XLA Modules:
  0.0 29.9 jit_solution(743651616865357354)
XLA Ops:
  0.7 28.5 %shard_map.64 = bf16[256,1024]{1,0:T(8,128)(2,1)S(1)} custom-call(s32[1]{0:T(128)S(6)} %copy.8.len_ref, s32[1,32]{1,0:T(1,128)} %pos_hbm.1, bf16[256,1024]{1,0:T(8,128)(2,1)} %q_hbm.1, bf16[256,256]{1,0:T(8,128)(2,1)} %k_hbm.1, bf16[256,256]{1,0:T(8,128)(2,1)} %v_hbm.1, bf16[1024,4096]{1,0:T(8,128)(2,1)} %w_hbm.1), custom_call_target="tpu_custom_call" | custom-call | tf_op jit(solution)/shard_map/pallas_call | solution.py:332
  29.1 0.8 %copy.9 = bf16[256,1024]{1,0:T(8,128)(2,1)} copy(bf16[256,1024]{1,0:T(8,128)(2,1)S(1)} %shard_map.64) | data formatting | bytes 1048576

commit v7 on v4

--- a/solution.py
+++ b/solution.py
@@ -108,7 +108,7 @@
     def anchor_copy(i, origin):
         rows = pl.ds(0, ANCHOR)
         if i < kv_heads:
-            source, target, lanes = k_v, rem_k, key_lanes(i)
+            source, target, lanes = k_hbm, rem_k, key_lanes(i)
         else:
             source, target, lanes = v_v, rem_v, val_lanes(i - kv_heads)
         return pltpu.make_async_remote_copy(
@@ -117,8 +117,6 @@
             device_id={"ctx": lax.rem(me_c + 1, n_ctx)}, device_id_type=MESH,
         )
 
-    for copy in loads:
-        copy.wait()
     @pl.when(me_c < n_ctx - 1)
     def _():
         pl.semaphore_wait(barrier, steps + 1)
@@ -135,6 +133,8 @@
                     anchor_copy(i, True).start()
 
     start_anchor(0, kv_heads)
+    for copy in loads:
+        copy.wait()
     picked = lax.broadcasted_iota(jnp.int32, (tok, retained), 0) == pos_v[...]
     picked = picked.astype(jnp.bfloat16)
     mine = pl.ds(pl.multiple_of(ANCHOR + me_c * retained, retained), retained)

time: 29.4 us -> 29.6 us (level)
  no operation moved by 1% of the time
where the time goes in v7:
time: 29.6 us; the launch traced here: 29.4 us
  Pallas kernels  28 us (95%)
  local copies, waits for them, and re-layouts  0.8 us (3%)
  between operations  0.66 us (2%)
    pallas_call x1, Pallas kernels, local(): pl.pallas_call(functools.partial(kernel, n_ctx, n_head), out_shape=jax.Sh...  28 us
    unnamed x1, local copies, waits for them, and re-layouts  0.8 us

profile of v7, /device:TPU:25, one launch (start us, length us, event | category | flops | bytes accessed | tf_op | source)
XLA Modules:
  0.0 29.4 jit_solution(12351234802778311359)
XLA Ops:
  0.7 28.0 %shard_map.64 = bf16[256,1024]{1,0:T(8,128)(2,1)S(1)} custom-call(s32[1]{0:T(128)S(6)} %copy.8.len_ref, s32[1,32]{1,0:T(1,128)} %pos_hbm.1, bf16[256,1024]{1,0:T(8,128)(2,1)} %q_hbm.1, bf16[256,256]{1,0:T(8,128)(2,1)} %k_hbm.1, bf16[256,256]{1,0:T(8,128)(2,1)} %v_hbm.1, bf16[1024,4096]{1,0:T(8,128)(2,1)} %w_hbm.1), custom_call_target="tpu_custom_call" | custom-call | tf_op jit(solution)/shard_map/pallas_call | solution.py:333
  28.6 0.8 %copy.9 = bf16[256,1024]{1,0:T(8,128)(2,1)} copy(bf16[256,1024]{1,0:T(8,128)(2,1)S(1)} %shard_map.64) | data formatting | bytes 1048576

commit v8 on v4

--- a/solution.py
+++ b/solution.py
@@ -48,7 +48,7 @@
     chunks, _, chunk = part.shape
     slab = chunks * chunk
     half = tok // 2
-    pieces = 2 * kv_heads
+    pieces = 3 * kv_heads
 
     def key_lanes(k):
         return pl.ds(k * HEAD_SIZE, HEAD_SIZE)
@@ -110,7 +110,8 @@
         if i < kv_heads:
             source, target, lanes = k_v, rem_k, key_lanes(i)
         else:
-            source, target, lanes = v_v, rem_v, val_lanes(i - kv_heads)
+            source, target, lanes = v_v, rem_v, val_lanes((i - kv_heads) // 2)
+            rows = pl.ds((i - kv_heads) % 2 * (ANCHOR // 2), ANCHOR // 2)
         return pltpu.make_async_remote_copy(
             src_ref=(source if origin else target).at[rows, lanes], dst_ref=target.at[rows, lanes],
             send_sem=anc_send.at[i], recv_sem=anc_recv.at[i],
@@ -192,8 +193,9 @@
 
         @pl.when((me_c > 0) & (me_c < n_ctx - 1))
         def _():
-            anchor_copy(number, False).wait_recv()
-            anchor_copy(number, False).start()
+            for i in [number] if number < kv_heads else [2 * number - kv_heads, 2 * number - kv_heads + 1]:
+                anchor_copy(i, False).wait_recv()
+                anchor_copy(i, False).start()
 
         if number == kv_heads - 1 and n_ctx > 1:
             forward_pass(0)
@@ -205,8 +207,8 @@
                 copies = pass_copies(source)
                 for copy in copies[1:] if values else copies[:1]:
                     copy.wait_recv()
-            for k in range(kv_heads):
-                anchor_copy(k + values * kv_heads, False).wait_recv()
+            for i in range(kv_heads, pieces) if values else range(kv_heads):
+                anchor_copy(i, False).wait_recv()
 
     await_remote(0)
     place = lax.broadcasted_iota(jnp.int32, (1, rem_rows), 1)
@@ -354,8 +356,8 @@
             dma((n_head,)),
             dma((n_ctx, 1 + kv_heads)),
             dma((n_ctx, 1 + kv_heads)),
-            dma((2 * kv_heads,)),
-            dma((2 * kv_heads,)),
+            dma((3 * kv_heads,)),
+            dma((3 * kv_heads,)),
             dma((n_head - 1, chunks, 2)),
             dma((n_head - 1, chunks, 2)),
         ],

time: 29.4 us -> 29.4 us (level)
  no operation moved by 1% of the time
where the time goes in v8:
time: 29.4 us; the launch traced here: 29.3 us
  Pallas kernels  27.8 us (95%)
  local copies, waits for them, and re-layouts  0.8 us (3%)
  between operations  0.66 us (2%)
    pallas_call x1, Pallas kernels, local(): pl.pallas_call(functools.partial(kernel, n_ctx, n_head), out_shape=jax.Sh...  27.8 us
    unnamed x1, local copies, waits for them, and re-layouts  0.8 us

profile of v8, /device:TPU:25, one launch (start us, length us, event | category | flops | bytes accessed | tf_op | source)
XLA Modules:
  0.0 29.3 jit_solution(11319428392067101630)
XLA Ops:
  0.7 27.8 %shard_map.64 = bf16[256,1024]{1,0:T(8,128)(2,1)S(1)} custom-call(s32[1]{0:T(128)S(6)} %copy.8.len_ref, s32[1,32]{1,0:T(1,128)} %pos_hbm.1, bf16[256,1024]{1,0:T(8,128)(2,1)} %q_hbm.1, bf16[256,256]{1,0:T(8,128)(2,1)} %k_hbm.1, bf16[256,256]{1,0:T(8,128)(2,1)} %v_hbm.1, bf16[1024,4096]{1,0:T(8,128)(2,1)} %w_hbm.1), custom_call_target="tpu_custom_call" | custom-call | tf_op jit(solution)/shard_map/pallas_call | solution.py:335
  28.5 0.8 %copy.9 = bf16[256,1024]{1,0:T(8,128)(2,1)} copy(bf16[256,1024]{1,0:T(8,128)(2,1)S(1)} %shard_map.64) | data formatting | bytes 1048576

commit v9 on v4

--- a/solution.py
+++ b/solution.py
@@ -319,7 +319,7 @@
     retained = retained_positions.shape[1]
     rem_rows = pl.cdiv(ANCHOR + n_ctx * retained, HEAD_SIZE) * HEAD_SIZE
     slab = out_proj.shape[1] // n_head
-    chunk = math.gcd(slab, 256)
+    chunk = math.gcd(slab, 512)
     chunks = slab // chunk
     dma = pltpu.SemaphoreType.DMA
     held = pl.BlockSpec(memory_space=pltpu.HBM)

time: 29.4 us -> 29.2 us (level)
  no operation moved by 1% of the time
where the time goes in v9:
time: 29.2 us; the launch traced here: 29.1 us
  Pallas kernels  27.6 us (95%)
  local copies, waits for them, and re-layouts  0.8 us (3%)
  between operations  0.66 us (2%)
    pallas_call x1, Pallas kernels, local(): pl.pallas_call(functools.partial(kernel, n_ctx, n_head), out_shape=jax.Sh...  27.6 us
    unnamed x1, local copies, waits for them, and re-layouts  0.8 us

profile of v9, /device:TPU:25, one launch (start us, length us, event | category | flops | bytes accessed | tf_op | source)
XLA Modules:
  0.0 29.1 jit_solution(554781200561941150)
XLA Ops:
  0.7 27.6 %shard_map.64 = bf16[256,1024]{1,0:T(8,128)(2,1)S(1)} custom-call(s32[1]{0:T(128)S(6)} %copy.8.len_ref, s32[1,32]{1,0:T(1,128)} %pos_hbm.1, bf16[256,1024]{1,0:T(8,128)(2,1)} %q_hbm.1, bf16[256,256]{1,0:T(8,128)(2,1)} %k_hbm.1, bf16[256,256]{1,0:T(8,128)(2,1)} %v_hbm.1, bf16[1024,4096]{1,0:T(8,128)(2,1)} %w_hbm.1), custom_call_target="tpu_custom_call" | custom-call | tf_op jit(solution)/shard_map/pallas_call | solution.py:333
  28.3 0.8 %copy.9 = bf16[256,1024]{1,0:T(8,128)(2,1)} copy(bf16[256,1024]{1,0:T(8,128)(2,1)S(1)} %shard_map.64) | data formatting | bytes 1048576
